TPU v7x, 256 devices: a whole 4x4x8 slice. The times are simulated.
256 devices in a mesh: cuts: 4 (over z_hi), fsdp: 32 (over x, y, core), dp: 2 (over z_lo).
Axes of the slice: x: 4, y: 4, z: 8 (z_hi: 4, z_lo: 2; z = z_hi * 2 + z_lo), core: 2. Of those that a mesh axis runs over, the one named last changes fastest.
Arguments:
- grads: float32 [256, 1048576], P(('cuts', 'fsdp', 'dp')), may hold values from -0.9765625 to 0.9765625, as said below
- residual: float32 [4, 1048576], P('cuts', ('fsdp', 'dp')), may hold values from -0.125 to 0.125, as said below
- master: float32 [1048576], P(('fsdp', 'dp')), may hold values from -6 to 6
- moment_one: float32 [1048576], P(('fsdp', 'dp')), may hold values from -6 to 6
- moment_two: float32 [1048576], P(('fsdp', 'dp')), may hold values from 0.1 to 10
Outputs:
- params: bfloat16 [1048576], replicated
- new_master: float32 [1048576], P(('fsdp', 'dp'))
- new_moment_one: float32 [1048576], P(('fsdp', 'dp'))
- new_moment_two: float32 [1048576], P(('fsdp', 'dp'))
- new_residual: float32 [4, 1048576], P('cuts', ('fsdp', 'dp'))
Inputs may be any that keep to these rules, and one draw needn't show every extreme that they name: `grads`: every entry is a whole multiple of 2^-8. `residual`: every entry is a whole multiple of 2^-12.
All inputs are finite; a program needn't handle non-finite values.
Results may differ from a plain program's by a relative error of at most 0.015.
Values may be sent and summed in bfloat16 or wider, within the bound.
No kernel may reach another device: no remote copies, remote signals or barrier semaphores. Data moves between devices by JAX's collectives and lax.ppermute only.
A program may use at most 64 MiB of HBM per device.

v0:
```python
import jax
import jax.numpy as jnp
from jax import lax
from jax.sharding import PartitionSpec as P

STEP = 10


def on_device(grads, residual, master, moment_one, moment_two):
    local = grads[0]
    slice_sum = lax.psum_scatter(local, ("fsdp", "dp"), scatter_dimension=0, tiled=True)
    corrected = slice_sum + residual[0]
    sent = jnp.floor(corrected * 4.0 + 0.5) * 0.25
    new_residual = (corrected - sent)[None, :]
    gradient = lax.psum(sent.astype(jnp.bfloat16), "cuts").astype(jnp.float32)
    new_moment_one = 0.9 * moment_one + 0.1 * gradient
    new_moment_two = 0.95 * moment_two + 0.05 * gradient * gradient
    first_hat = new_moment_one / (1.0 - 0.9**STEP)
    second_hat = new_moment_two / (1.0 - 0.95**STEP)
    new_master = master - 0.003 * (first_hat / (jnp.sqrt(second_hat) + 1e-08) + 0.1 * master)
    rounded = new_master.astype(jnp.bfloat16)
    params = lax.all_gather(rounded, ("fsdp", "dp"), axis=0, tiled=True)
    return (params, new_master, new_moment_one, new_moment_two, new_residual)


def solution(mesh):
    placed = (
        P(("cuts", "fsdp", "dp"), None),
        P("cuts", ("fsdp", "dp")),
        P(("fsdp", "dp")),
        P(("fsdp", "dp")),
        P(("fsdp", "dp")),
    )
    return jax.shard_map(
        on_device,
        mesh=mesh,
        in_specs=placed,
        out_specs=(
            P(),
            P(("fsdp", "dp")),
            P(("fsdp", "dp")),
            P(("fsdp", "dp")),
            P("cuts", ("fsdp", "dp")),
        ),
        check_vma=False,
    )
```

profile of v0, /device:TPU:1, one launch (start us, length us, event | category | flops | bytes accessed | tf_op | source)
XLA Modules:
  0.0 772.8 jit_solution(2088208545626012807)
XLA Ops:
  7.2 0.0 copy-start.4
  7.2 0.0 copy-start
  7.2 0.0 copy-start.1
  7.2 0.0 copy-start.2
  7.2 0.0 copy-start.3
  7.2 0.0 all-reduce.3.cloned.1.call-start
  7.3 0.7 all-reduce.3.cloned.1.call-update
  8.0 0.0 all-gather.2.cloned.1.call-start
  8.0 0.0 copy-done.4
  8.0 0.6 dynamic-slice
  9.3 578.8 %all-reduce.3.cloned.1.call-done = f32[1048576]{0:T(1024)} async-done(((f32[1048576]{0:T(1024)}), f32[1048576]{0:T(1024)}) %all-reduce.3.cloned.1.call-update) | async-done | bytes 4194320
  588.1 0.0 copy-done
  588.1 1.5 fusion.2
  589.6 15.6 %psum.7 = bf16[16384]{0:T(1024)(128)(2,1)S(1)} all-reduce(bf16[16384]{0:T(1024)(128)(2,1)S(1)} %get-tuple-element.10), channel_id=1, replica_groups=mesh['cuts'=4,'fsdp'=32,'dp'=2] {'cuts'}, use_global_device_ids=true, to_apply=%region_1.0 | all-reduce | flops 16384 | bytes 65536 | tf_op jit(solution)/shard_map/psum | solution.py:15
  605.2 0.0 copy-done.1
  605.2 0.0 copy-done.2
  605.2 0.0 copy-done.3
  605.2 0.7 fusion.4
  605.9 0.0 all-gather.2.cloned.1.call-update
  605.9 157.0 %all-gather.2.cloned.1.call-done = bf16[1048576]{0:T(1024)(128)(2,1)} async-done(((bf16[16384]{0:T(1024)(128)(2,1)}), bf16[1048576]{0:T(1024)(128)(2,1)}) %all-gather.2.cloned.1.call-update) | async-done | bytes 2097168 | tf_op jit(solution)/shard_map/all_gather | solution.py:22
  762.9 3.0 copy.13
Async XLA Ops:
  7.2 0.8 copy-start.4
  7.2 580.9 %copy-start = (f32[1,16384]{1,0:T(1,128)S(1)}, f32[1,16384]{1,0:T(1,128)}, u32[]{:S(2)}) copy-start(f32[1,16384]{1,0:T(1,128)} %param.6) | copy-start | bytes 196612
  7.2 598.0 %copy-start.1 = (f32[16384]{0:T(1024)S(1)}, f32[16384]{0:T(1024)}, u32[]{:S(2)}) copy-start(f32[16384]{0:T(1024)} %param.7) | copy-start | bytes 196612
  7.2 598.0 %copy-start.2 = (f32[16384]{0:T(1024)S(1)}, f32[16384]{0:T(1024)}, u32[]{:S(2)}) copy-start(f32[16384]{0:T(1024)} %param.8) | copy-start | bytes 196612
  7.2 598.0 %copy-start.3 = (f32[16384]{0:T(1024)S(1)}, f32[16384]{0:T(1024)}, u32[]{:S(2)}) copy-start(f32[16384]{0:T(1024)} %param.9) | copy-start | bytes 196612
  7.2 580.9 %all-reduce.3.cloned.1.call-start = ((), (), s32[]{:S(2)}) async-start(), calls=%async_computation.1 | async-start | bytes 8388608
  8.0 755.0 %all-gather.2.cloned.1.call-start = ((), (), s32[]{:S(2)}) async-start(), calls=%async_computation | async-start | bytes 2129920 | tf_op jit(solution)/shard_map/all_gather | solution.py:22
Sparse Core Ops, SparseCore 0:
  10.7 577.3 all-reduce.2
  606.1 156.8 all-gather.1
where the time goes:
time: 773 us
  waiting for transfers between devices  737 us (95%)
  blocking collectives  15.6 us (2%)
  between operations  14.8 us (2%)
    unnamed x3, waiting for transfers between devices  580 us
    all_gather x1, waiting for transfers between devices, on_device(): params = lax.all_gather(rounded, ('fsdp', 'dp'), axis=0, tiled=True)  157 us
    psum x1, blocking collectives, on_device(): gradient = lax.psum(sent.astype(jnp.bfloat16), 'cuts').astype(jnp.float32)  15.6 us
  transfers between devices with their start and end apart: 2, of which 2 were waited for; matrix products, arithmetic and copies ran while one was open for 0% of the time, Pallas kernels for 0%

commit v1 on v0

v1 whole, which is shorter than its diff:
```python
import jax
import jax.numpy as jnp
from jax import lax
from jax.experimental import pallas as pl
from jax.experimental.pallas import tpu as pltpu
from jax.sharding import Mesh, PartitionSpec as P

STEP = 10
OWN = ("x", "y", "core", "dp")
CHIPS = ("x", "y", "dp")
TILE = (128, 128)
ROWS = 4


def narrow_kernel(core_ref, grads_ref, out_ref):
    out_ref[...] = grads_ref[:, 0].astype(jnp.bfloat16)


def narrow_other(core, grads):
    return pl.pallas_call(
        narrow_kernel,
        grid_spec=pltpu.PrefetchScalarGridSpec(
            num_scalar_prefetch=1,
            grid=(16 // ROWS,),
            in_specs=[pl.BlockSpec((ROWS, 1, 2, *TILE), lambda i, core: (i, 1 - core[0], 0, 0, 0))],
            out_specs=pl.BlockSpec((ROWS, 2, *TILE), lambda i, core: (i, 0, 0, 0)),
        ),
        out_shape=jax.ShapeDtypeStruct((16, 2, *TILE), jnp.bfloat16),
        name="narrow_other",
    )(core, grads)


def pair_kernel(core_ref, grads_ref, other_ref, out_ref):
    total = grads_ref[:, 0] + other_ref[...].astype(jnp.float32)
    inner = jnp.clip(total, -1.0, 1.0)
    out_ref[...] = jnp.where(total == inner, total, (total - inner) * 1024.0).astype(jnp.bfloat16)


def pair_sum(core, grads, other):
    return pl.pallas_call(
        pair_kernel,
        grid_spec=pltpu.PrefetchScalarGridSpec(
            num_scalar_prefetch=1,
            grid=(16 // ROWS,),
            in_specs=[
                pl.BlockSpec((ROWS, 1, 2, *TILE), lambda i, core: (i, core[0], 0, 0, 0)),
                pl.BlockSpec((ROWS, 2, *TILE), lambda i, core: (i, 0, 0, 0)),
            ],
            out_specs=pl.BlockSpec((ROWS, 2, *TILE), lambda i, core: (i, 0, 0, 0)),
        ),
        out_shape=jax.ShapeDtypeStruct((16, 2, *TILE), jnp.bfloat16),
        name="pair_sum",
    )(core, grads, other)


def decoded(code):
    code = code.astype(jnp.float32)
    return jnp.where(jnp.abs(code) > 2.0, code * (1.0 / 1024.0) + jnp.clip(code, -1.0, 1.0), code)


def on_device(grads, residual, master, moment_one, moment_two):
    core = lax.axis_index("core").reshape(1)
    swap = [(0, 1), (1, 0)]
    blocks = grads.reshape(16, 2, 2, *TILE)
    other = lax.ppermute(narrow_other(core, blocks), "core", swap)
    outgoing = pair_sum(core, blocks, other).reshape(32, *TILE)
    arrived = lax.all_to_all(outgoing, CHIPS, 0, 0, tiled=True)
    slice_sum = jnp.sum(decoded(arrived), axis=0)
    corrected = slice_sum + residual.reshape(TILE)
    sent = jnp.floor(corrected * 4.0 + 0.5) * 0.25
    new_residual = (corrected - sent).reshape(1, 16384)
    narrow = sent.astype(jnp.bfloat16)
    gradient = sent
    for shift in (1, 2, 3):
        gradient += lax.ppermute(narrow, "cuts", [(i, (i + shift) % 4) for i in range(4)]).astype(jnp.float32)
    master = master.reshape(TILE)
    new_moment_one = 0.9 * moment_one.reshape(TILE) + 0.1 * gradient
    new_moment_two = 0.95 * moment_two.reshape(TILE) + 0.05 * gradient * gradient
    first_hat = new_moment_one / (1.0 - 0.9**STEP)
    second_hat = new_moment_two / (1.0 - 0.95**STEP)
    new_master = master - 0.003 * (first_hat / (jnp.sqrt(second_hat) + 1e-08) + 0.1 * master)
    rounded = new_master.astype(jnp.bfloat16)
    mine = lax.all_to_all(jnp.broadcast_to(rounded, (32, *TILE)), CHIPS, 0, 0, tiled=True)
    theirs = lax.ppermute(mine, "core", swap)
    mine, theirs = mine.reshape(16, 2, *TILE), theirs.reshape(16, 2, *TILE)
    first = core[0] == 0
    params = jnp.stack([jnp.where(first, mine, theirs), jnp.where(first, theirs, mine)], axis=1)
    return (params.reshape(-1), new_master.reshape(-1), new_moment_one.reshape(-1), new_moment_two.reshape(-1), new_residual)


def solution(mesh):
    mesh = Mesh(mesh.devices.reshape(4, 4, 4, 2, 2), ("cuts",) + OWN)
    own = P(OWN)
    return jax.shard_map(
        on_device,
        mesh=mesh,
        in_specs=(P(("cuts",) + OWN, None), P("cuts", OWN), own, own, own),
        out_specs=(P(), own, own, own, P("cuts", OWN)),
        check_vma=False,
    )
```

time: 773 us -> 80.9 us (0.10)
  waiting for transfers between devices: 737 us -> 23.4 us
  starting transfers between devices: 0.08 us -> 18.5 us
  between operations: 14.8 us -> 0.69 us
  blocking collectives: 15.6 us -> 23.8 us
    unnamed x3 -> x0, waiting for transfers between devices: 580 us -> none
    all_gather x1 -> x0, waiting for transfers between devices: 157 us -> none  [on_device(): params = lax.all_gather(rounded, ('fsdp', 'dp'), axis=0, tiled=True)]
    all_to_all x0 -> x1, blocking collectives: none -> 23.8 us  [on_device(): arrived = lax.all_to_all(outgoing, CHIPS, 0, 0, tiled=True)]
    all_to_all x0 -> x1, waiting for transfers between devices: none -> 15.9 us  [on_device(): lax.all_to_all(jnp.broadcast_to(rounded, (32, *TILE)), CHIPS, 0, 0, tiled...]
    psum x1 -> x0, blocking collectives: 15.6 us -> none  [on_device(): gradient = lax.psum(sent.astype(jnp.bfloat16), 'cuts').astype(jnp.float32)]
    ppermute x0 -> x5, starting transfers between devices: none -> 14.6 us  [the longest x3 8.45 us: on_device(): lax.ppermute(narrow, 'cuts', [(i, (i + shift) % 4) for i in range(4)])]
  transfers between devices with their start and end apart: 2 -> 6, of which waited for: 2 -> 4; matrix products, arithmetic and copies ran while one was open for 0% -> 1% of each run, Pallas kernels for 0% -> 0%
where the time goes in v1:
time: 80.9 us; the launch traced here: 80.4 us
  blocking collectives  23.8 us (29%)
  waiting for transfers between devices  23.4 us (29%)
  starting transfers between devices  18.5 us (23%)
  Pallas kernels  7.55 us (9%)
  other arithmetic  4.31 us (5%)
  local copies, waits for them, and re-layouts  2.19 us (3%)
    all_to_all x1, blocking collectives, on_device(): arrived = lax.all_to_all(outgoing, CHIPS, 0, 0, tiled=True)  23.8 us
    all_to_all x1, waiting for transfers between devices, on_device(): lax.all_to_all(jnp.broadcast_to(rounded, (32, *TILE)), CHIPS, 0, 0, tiled...  15.9 us
    ppermute x3, starting transfers between devices, on_device(): lax.ppermute(narrow, 'cuts', [(i, (i + shift) % 4) for i in range(4)])  8.45 us
    pallas_call x1, Pallas kernels, pair_sum(): pl.pallas_call(pair_kernel, grid_spec=pltpu.PrefetchScalarGridSpec(num_sc...  3.95 us
    all_to_all x1, starting transfers between devices, on_device(): lax.all_to_all(jnp.broadcast_to(rounded, (32, *TILE)), CHIPS, 0, 0, tiled...  3.93 us
    pallas_call x1, Pallas kernels, narrow_other(): pl.pallas_call(narrow_kernel, grid_spec=pltpu.PrefetchScalarGridSpec(num_...  3.6 us
    ppermute x3, waiting for transfers between devices, on_device(): lax.ppermute(narrow, 'cuts', [(i, (i + shift) % 4) for i in range(4)])  3.42 us
    ppermute x1, starting transfers between devices, on_device(): other = lax.ppermute(narrow_other(core, blocks), 'core', swap)  3.24 us
  transfers between devices with their start and end apart: 6, of which 4 were waited for; matrix products, arithmetic and copies ran while one was open for 1% of the time, Pallas kernels for 0%

profile of v1, /device:TPU:1, one launch (start us, length us, event | category | flops | bytes accessed | tf_op | source)
XLA Modules:
  0.0 80.4 jit_solution(10104606855471625695)
XLA Ops:
  0.6 3.6 %narrow_other.1 = bf16[16,2,128,128]{3,2,1,0:T(8,128)(2,1)} custom-call(s32[1]{0:T(128)} %bitcast.2.core_ref, f32[16,2,2,128,128]{4,3,2,1,0:T(8,128)} %bitcast.37), custom_call_target="tpu_custom_call" | custom-call | tf_op jit(solution)/shard_map/narrow_other/pallas_call | solution.py:20
  4.2 3.2 %collective-permute-start = (bf16[16,2,128,128]{3,2,1,0:T(8,128)(2,1)}, bf16[16,2,128,128]{3,2,1,0:T(8,128)(2,1)S(1)}, u32[]{:S(2)}, u32[]{:S(2)}) collective-permute-start(bf16[16,2,128,128]{3,2,1,0:T(8,128)(2,1)} %narrow_other.1), channel_id=1, source_target_pairs={{0,2},{2,0},{1,3},{3,1},{4,6},{6,4},{5,7},{7,5},{8,10},{10,8},{9,1... | collective-permute-start | bytes 3145736 | tf_op jit(solution)/shard_map/ppermute | solution.py:65
  7.5 2.5 %collective-permute-done.other_ref = bf16[16,2,128,128]{3,2,1,0:T(8,128)(2,1)S(1)} collective-permute-done((bf16[16,2,128,128]{3,2,1,0:T(8,128)(2,1)}, bf16[16,2,128,128]{3,2,1,0:T(8,128)(2,1)S(1)}, u32[]{:S(2)}, u32[]{:S(2)}) %collective-permute-start) | collective-permute-done | bytes 1048608 | tf_op jit(solution)/shard_map/ppermute | solution.py:65
  10.0 0.0 copy-start
  10.0 1.0 %copy-done = bf16[16,2,128,128]{3,2,1,0:T(8,128)(2,1)} copy-done((bf16[16,2,128,128]{3,2,1,0:T(8,128)(2,1)}, bf16[16,2,128,128]{3,2,1,0:T(8,128)(2,1)S(1)}, u32[]{:S(2)}) %copy-start) | copy-done | bytes 1048600
  10.9 4.0 %pair_sum.1 = bf16[16,2,128,128]{3,2,1,0:T(8,128)(2,1)} custom-call(s32[1]{0:T(128)} %bitcast.2.core_ref, f32[16,2,2,128,128]{4,3,2,1,0:T(8,128)} %bitcast.38, bf16[16,2,128,128]{3,2,1,0:T(8,128)(2,1)} %copy-done), custom_call_target="tpu_custom_call" | custom-call | tf_op jit(solution)/shard_map/pair_sum/pallas_call | solution.py:40
  14.9 0.0 copy-start.1
  14.9 0.0 copy-start.2
  14.9 0.0 copy-start.3
  14.9 0.0 copy-start.4
  14.9 23.8 %all_to_all.10 = bf16[32,128,128]{2,1,0:T(8,128)(2,1)S(1)} all-to-all(bf16[32,128,128]{2,1,0:T(8,128)(2,1)} %bitcast.39), channel_id=1, replica_groups=mesh['cuts'=4,'x'=4,'y'=4,'core'=2,'dp'=2] {'x','y','dp'}, dimensions={0} | all-to-all | bytes 2097152 | tf_op jit(solution)/shard_map/all_to_all | solution.py:67
  38.7 0.5 fusion.2
  39.3 0.0 copy-done.1
  39.3 5.2 %collective-permute-start.3 = (bf16[128,128]{1,0:T(8,128)(2,1)S(1)}, bf16[128,128]{1,0:T(8,128)(2,1)S(1)}, u32[]{:S(2)}, u32[]{:S(2)}) collective-permute-start(bf16[128,128]{1,0:T(8,128)(2,1)S(1)} %fusion.8), channel_id=1, source_target_pairs={{0,192},{64,0},{128,64},{192,128},{1,193},{65,1},{129,65},{193,129... | collective-permute-start | bytes 98312 | tf_op jit(solution)/shard_map/ppermute | solution.py:75
  44.5 1.2 %collective-permute-start.2 = (bf16[128,128]{1,0:T(8,128)(2,1)S(1)}, bf16[128,128]{1,0:T(8,128)(2,1)S(1)}, u32[]{:S(2)}, u32[]{:S(2)}) collective-permute-start(bf16[128,128]{1,0:T(8,128)(2,1)S(1)} %fusion.8), channel_id=1, source_target_pairs={{0,128},{64,192},{128,0},{192,64},{1,129},{65,193},{129,1},{193,65... | collective-permute-start | bytes 98312 | tf_op jit(solution)/shard_map/ppermute | solution.py:75
  45.7 2.1 %collective-permute-start.1 = (bf16[128,128]{1,0:T(8,128)(2,1)S(1)}, bf16[128,128]{1,0:T(8,128)(2,1)S(1)}, u32[]{:S(2)}, u32[]{:S(2)}) collective-permute-start(bf16[128,128]{1,0:T(8,128)(2,1)S(1)} %fusion.8), channel_id=1, source_target_pairs={{0,64},{64,128},{128,192},{192,0},{1,65},{65,129},{129,193},{193,1... | collective-permute-start | bytes 98312 | tf_op jit(solution)/shard_map/ppermute | solution.py:75
  47.8 0.0 collective-permute-done.3
  47.8 3.4 %collective-permute-done.2 = bf16[128,128]{1,0:T(8,128)(2,1)S(1)} collective-permute-done((bf16[128,128]{1,0:T(8,128)(2,1)S(1)}, bf16[128,128]{1,0:T(8,128)(2,1)S(1)}, u32[]{:S(2)}, u32[]{:S(2)}) %collective-permute-start.2) | collective-permute-done | bytes 32800 | tf_op jit(solution)/shard_map/ppermute | solution.py:75
  51.2 0.0 collective-permute-done.1
  51.2 0.0 copy-done.2
  51.2 0.7 fusion.7
  51.9 0.0 copy-done.3
  51.9 0.0 copy-done.4
  51.9 0.7 fusion.9
  52.6 1.2 %broadcast_in_dim.3 = bf16[32,128,128]{2,1,0:T(8,128)(2,1)} broadcast(bf16[128,128]{1,0:T(8,128)(2,1)S(1)} %get-tuple-element.7), dimensions={1,2} | broadcast | bytes 1081344 | tf_op jit(solution)/shard_map/broadcast_in_dim | solution.py:83
  53.8 3.9 %all-to-all-start.1 = ((bf16[32,128,128]{2,1,0:T(8,128)(2,1)}), bf16[32,128,128]{2,1,0:T(8,128)(2,1)S(1)}, u32[]{:S(2)}, u32[]{:S(2)}) async-start(bf16[32,128,128]{2,1,0:T(8,128)(2,1)} %broadcast_in_dim.3), calls=%async_computation.1 | async-start | bytes 2097152 | tf_op jit(solution)/shard_map/all_to_all | solution.py:83
  57.7 15.9 %all-to-all-done.1 = bf16[32,128,128]{2,1,0:T(8,128)(2,1)S(1)} async-done(((bf16[32,128,128]{2,1,0:T(8,128)(2,1)}), bf16[32,128,128]{2,1,0:T(8,128)(2,1)S(1)}, u32[]{:S(2)}, u32[]{:S(2)}) %all-to-all-start.1) | async-done | bytes 1048608 | tf_op jit(solution)/shard_map/all_to_all | solution.py:83
  73.6 2.9 %collective-permute-start.4 = (bf16[32,128,128]{2,1,0:T(8,128)(2,1)S(1)}, bf16[32,128,128]{2,1,0:T(8,128)(2,1)S(1)}, u32[]{:S(2)}, u32[]{:S(2)}) collective-permute-start(bf16[32,128,128]{2,1,0:T(8,128)(2,1)S(1)} %all-to-all-done.1), channel_id=1, source_target_pairs={{0,2},{2,0},{1,3},{3,1},{4,6},{6,4},{5,7},{7,5},{8,10},{10,8},{9,1... | collective-permute-start | bytes 3145736 | tf_op jit(solution)/shard_map/ppermute | solution.py:84
  76.5 0.7 multiply_subtract_fusion
  77.2 1.5 %collective-permute-done.4 = bf16[32,128,128]{2,1,0:T(8,128)(2,1)S(1)} collective-permute-done((bf16[32,128,128]{2,1,0:T(8,128)(2,1)S(1)}, bf16[32,128,128]{2,1,0:T(8,128)(2,1)S(1)}, u32[]{:S(2)}, u32[]{:S(2)}) %collective-permute-start.4) | collective-permute-done | bytes 1048608 | tf_op jit(solution)/shard_map/ppermute | solution.py:84
  78.8 0.1 broadcast_select_fusion.1
  78.9 1.5 %pad_maximum_fusion = bf16[16,2,2,128,128]{4,3,2,1,0:T(8,128)(2,1)} fusion(bf16[16,1,2,128,128]{4,3,2,1,0:T(8,128)(2,1)S(1)} %bitcast.41, bf16[16,1,2,128,128]{4,3,2,1,0:T(8,128)(2,1)S(1)} %bitcast.40), kind=kLoop, calls=%fused_computation.7 | loop fusion | flops 1048576 | bytes 4194304 | tf_op jit(solution)/shard_map/stack | solution.py:87
  (1 shorter events, 0.0 us)
Async XLA Ops:
  4.2 5.7 %collective-permute-start = (bf16[16,2,128,128]{3,2,1,0:T(8,128)(2,1)}, bf16[16,2,128,128]{3,2,1,0:T(8,128)(2,1)S(1)}, u32[]{:S(2)}, u32[]{:S(2)}) collective-permute-start(bf16[16,2,128,128]{3,2,1,0:T(8,128)(2,1)} %narrow_other.1), channel_id=1, source_target_pairs={{0,2},{2,0},{1,3},{3,1},{4,6},{6,4},{5,7},{7,5},{8,10},{10,8},{9,1... | collective-permute-start | bytes 3145736 | tf_op jit(solution)/shard_map/ppermute | solution.py:65
  10.0 1.0 %copy-start = (bf16[16,2,128,128]{3,2,1,0:T(8,128)(2,1)}, bf16[16,2,128,128]{3,2,1,0:T(8,128)(2,1)S(1)}, u32[]{:S(2)}) copy-start(bf16[16,2,128,128]{3,2,1,0:T(8,128)(2,1)S(1)} %collective-permute-done.other_ref) | copy-start | bytes 3145732
  14.9 24.4 %copy-start.1 = (f32[1,16384]{1,0:T(1,128)S(1)}, f32[1,16384]{1,0:T(1,128)}, u32[]{:S(2)}) copy-start(f32[1,16384]{1,0:T(1,128)} %param.6) | copy-start | bytes 196612
  14.9 36.3 %copy-start.2 = (f32[16384]{0:T(1024)S(1)}, f32[16384]{0:T(1024)}, u32[]{:S(2)}) copy-start(f32[16384]{0:T(1024)} %param.9) | copy-start | bytes 196612
  14.9 37.0 %copy-start.3 = (f32[16384]{0:T(1024)S(1)}, f32[16384]{0:T(1024)}, u32[]{:S(2)}) copy-start(f32[16384]{0:T(1024)} %param.8) | copy-start | bytes 196612
  14.9 37.0 %copy-start.4 = (f32[16384]{0:T(1024)S(1)}, f32[16384]{0:T(1024)}, u32[]{:S(2)}) copy-start(f32[16384]{0:T(1024)} %param.7) | copy-start | bytes 196612
  39.3 8.5 %collective-permute-start.3 = (bf16[128,128]{1,0:T(8,128)(2,1)S(1)}, bf16[128,128]{1,0:T(8,128)(2,1)S(1)}, u32[]{:S(2)}, u32[]{:S(2)}) collective-permute-start(bf16[128,128]{1,0:T(8,128)(2,1)S(1)} %fusion.8), channel_id=1, source_target_pairs={{0,192},{64,0},{128,64},{192,128},{1,193},{65,1},{129,65},{193,129... | collective-permute-start | bytes 98312 | tf_op jit(solution)/shard_map/ppermute | solution.py:75
  44.5 6.7 %collective-permute-start.2 = (bf16[128,128]{1,0:T(8,128)(2,1)S(1)}, bf16[128,128]{1,0:T(8,128)(2,1)S(1)}, u32[]{:S(2)}, u32[]{:S(2)}) collective-permute-start(bf16[128,128]{1,0:T(8,128)(2,1)S(1)} %fusion.8), channel_id=1, source_target_pairs={{0,128},{64,192},{128,0},{192,64},{1,129},{65,193},{129,1},{193,65... | collective-permute-start | bytes 98312 | tf_op jit(solution)/shard_map/ppermute | solution.py:75
  45.7 5.5 %collective-permute-start.1 = (bf16[128,128]{1,0:T(8,128)(2,1)S(1)}, bf16[128,128]{1,0:T(8,128)(2,1)S(1)}, u32[]{:S(2)}, u32[]{:S(2)}) collective-permute-start(bf16[128,128]{1,0:T(8,128)(2,1)S(1)} %fusion.8), channel_id=1, source_target_pairs={{0,64},{64,128},{128,192},{192,0},{1,65},{65,129},{129,193},{193,1... | collective-permute-start | bytes 98312 | tf_op jit(solution)/shard_map/ppermute | solution.py:75
  53.8 19.8 %all-to-all-start.1 = ((bf16[32,128,128]{2,1,0:T(8,128)(2,1)}), bf16[32,128,128]{2,1,0:T(8,128)(2,1)S(1)}, u32[]{:S(2)}, u32[]{:S(2)}) async-start(bf16[32,128,128]{2,1,0:T(8,128)(2,1)} %broadcast_in_dim.3), calls=%async_computation.1 | async-start | bytes 2097152 | tf_op jit(solution)/shard_map/all_to_all | solution.py:83
  73.6 5.2 %collective-permute-start.4 = (bf16[32,128,128]{2,1,0:T(8,128)(2,1)S(1)}, bf16[32,128,128]{2,1,0:T(8,128)(2,1)S(1)}, u32[]{:S(2)}, u32[]{:S(2)}) collective-permute-start(bf16[32,128,128]{2,1,0:T(8,128)(2,1)S(1)} %all-to-all-done.1), channel_id=1, source_target_pairs={{0,2},{2,0},{1,3},{3,1},{4,6},{6,4},{5,7},{7,5},{8,10},{10,8},{9,1... | collective-permute-start | bytes 3145736 | tf_op jit(solution)/shard_map/ppermute | solution.py:84

commit v2 on v0

v2 whole, which is shorter than its diff:
```python
import jax
import jax.numpy as jnp
from jax import lax
from jax.sharding import Mesh, PartitionSpec as P

STEP = 10
OWN = ("x", "y", "core", "dp")
CHIPS = ("x", "y", "dp")
TILE = (128, 128)
SWAP = [(0, 1), (1, 0)]


def coded(total):
    inner = jnp.clip(total, -1.0, 1.0)
    return jnp.where(total == inner, total, (total - inner) * 1024.0).astype(jnp.bfloat16)


def decoded(code):
    code = code.astype(jnp.float32)
    return jnp.where(jnp.abs(code) > 2.0, code * (1.0 / 1024.0) + jnp.clip(code, -1.0, 1.0), code)


def on_device(grads, residual, master, moment_one, moment_two):
    core = lax.axis_index("core")
    blocks = lax.optimization_barrier(grads.reshape(16, 2, 2, *TILE))
    half = lambda blocks, which: lax.dynamic_index_in_dim(blocks, which, 1, False).astype(jnp.bfloat16)
    leaving = half(blocks, 1 - core)
    other = lax.ppermute(leaving, "core", SWAP)
    blocks, _ = lax.optimization_barrier((blocks, leaving))
    own = lax.optimization_barrier(half(blocks, core))
    total = own.astype(jnp.float32) + other.astype(jnp.float32)
    arrived = lax.all_to_all(coded(total).reshape(32, *TILE), CHIPS, 0, 0, tiled=True)
    slice_sum = jnp.sum(decoded(arrived), axis=0).reshape(-1)
    corrected = slice_sum + residual[0]
    sent = jnp.floor(corrected * 4.0 + 0.5) * 0.25
    new_residual = (corrected - sent)[None]
    narrow = sent.astype(jnp.bfloat16)
    sents = [lax.ppermute(narrow, "cuts", [(i, (i + shift) % 4) for i in range(4)]) for shift in (1, 2, 3)]
    new_residual, sents = lax.optimization_barrier((new_residual, sents))
    gradient = sent + sum(one.astype(jnp.float32) for one in sents)
    new_moment_one = 0.9 * moment_one + 0.1 * gradient
    new_moment_two = 0.95 * moment_two + 0.05 * gradient * gradient
    first_hat = new_moment_one / (1.0 - 0.9**STEP)
    second_hat = new_moment_two / (1.0 - 0.95**STEP)
    new_master = master - 0.003 * (first_hat / (jnp.sqrt(second_hat) + 1e-08) + 0.1 * master)
    rounded = new_master.astype(jnp.bfloat16).reshape(TILE)
    mine = lax.all_to_all(jnp.broadcast_to(rounded, (32, *TILE)), CHIPS, 0, 0, tiled=True)
    theirs = lax.ppermute(mine, "core", SWAP)
    place = lax.broadcasted_iota(jnp.int32, (1, 2, 1, 1, 1), 1)
    params = jnp.where(place == core, mine.reshape(16, 1, 2, *TILE), theirs.reshape(16, 1, 2, *TILE))
    return (params.reshape(-1), new_master, new_moment_one, new_moment_two, new_residual)


def solution(mesh):
    mesh = Mesh(mesh.devices.reshape(4, 4, 4, 2, 2), ("cuts",) + OWN)
    own = P(OWN)
    return jax.shard_map(
        on_device,
        mesh=mesh,
        in_specs=(P(("cuts",) + OWN, None), P("cuts", OWN), own, own, own),
        out_specs=(P(), own, own, own, P("cuts", OWN)),
        check_vma=False,
    )
```

time: 773 us -> 72 us (0.09)
  waiting for transfers between devices: 737 us -> 5.49 us
  blocking collectives: 15.6 us -> 43.1 us
  starting transfers between devices: 0.08 us -> 14.6 us
  between operations: 14.8 us -> 0.73 us
    unnamed x3 -> x0, waiting for transfers between devices: 580 us -> none
    all_gather x1 -> x0, waiting for transfers between devices: 157 us -> none  [on_device(): params = lax.all_gather(rounded, ('fsdp', 'dp'), axis=0, tiled=True)]
    all_to_all x0 -> x2, blocking collectives: none -> 43.1 us  [the longest x1 23.6 us: on_device(): lax.all_to_all(coded(total).reshape(32, *TILE), CHIPS, 0, 0, tiled=True)]
    psum x1 -> x0, blocking collectives: 15.6 us -> none  [on_device(): gradient = lax.psum(sent.astype(jnp.bfloat16), 'cuts').astype(jnp.float32)]
    ppermute x0 -> x5, starting transfers between devices: none -> 14.6 us  [the longest x3 8.45 us: on_device(): lax.ppermute(narrow, 'cuts', [(i, (i + shift) % 4) for i in range(4)])]
  transfers between devices with their start and end apart: 2 -> 5, of which waited for: 2 -> 3; matrix products, arithmetic and copies ran while one was open for 0% -> 3% of each run, Pallas kernels for 0% -> 0%
where the time goes in v2:
time: 72 us; the launch traced here: 71.8 us
  blocking collectives  43.1 us (60%)
  starting transfers between devices  14.6 us (20%)
  waiting for transfers between devices  5.49 us (8%)
  other arithmetic  4.17 us (6%)
  local copies, waits for them, and re-layouts  3.76 us (5%)
  between operations  0.73 us (1%)
    all_to_all x1, blocking collectives, on_device(): lax.all_to_all(coded(total).reshape(32, *TILE), CHIPS, 0, 0, tiled=True)  23.6 us
    all_to_all x1, blocking collectives, on_device(): lax.all_to_all(jnp.broadcast_to(rounded, (32, *TILE)), CHIPS, 0, 0, tiled...  19.4 us
    ppermute x3, starting transfers between devices, on_device(): lax.ppermute(narrow, 'cuts', [(i, (i + shift) % 4) for i in range(4)])  8.45 us
    convert_element_type x2, local copies, waits for them, and re-layouts, on_device(): lax.dynamic_index_in_dim(blocks, which, 1, False).astype(jnp.bfloat16)  3.51 us
    ppermute x1, starting transfers between devices, on_device(): other = lax.ppermute(leaving, 'core', SWAP)  3.33 us
    ppermute x1, starting transfers between devices, on_device(): theirs = lax.ppermute(mine, 'core', SWAP)  2.79 us
    ppermute x3, waiting for transfers between devices, on_device(): lax.ppermute(narrow, 'cuts', [(i, (i + shift) % 4) for i in range(4)])  2.68 us
    ppermute x1, waiting for transfers between devices, on_device(): theirs = lax.ppermute(mine, 'core', SWAP)  2.28 us
  transfers between devices with their start and end apart: 5, of which 3 were waited for; matrix products, arithmetic and copies ran while one was open for 3% of the time, Pallas kernels for 0%

profile of v2, /device:TPU:1, one launch (start us, length us, event | category | flops | bytes accessed | tf_op | source)
XLA Modules:
  0.0 71.8 jit_solution(7337857229233110189)
XLA Ops:
  0.6 1.8 %fusion.6 = bf16[16,2,128,128]{3,2,1,0:T(8,128)(2,1)S(1)} fusion(f32[16,2,2,128,128]{4,3,2,1,0:T(8,128)} %bitcast.38, s32[]{:T(128)S(6)} %select_n.23), kind=kLoop, calls=%fused_computation.15 | loop fusion | bytes 2097156 | tf_op jit(solution)/shard_map/convert_element_type | solution.py:26
  2.4 3.3 %collective-permute-start = (bf16[16,2,128,128]{3,2,1,0:T(8,128)(2,1)S(1)}, bf16[16,2,128,128]{3,2,1,0:T(8,128)(2,1)S(1)}, u32[]{:S(2)}, u32[]{:S(2)}) collective-permute-start(bf16[16,2,128,128]{3,2,1,0:T(8,128)(2,1)S(1)} %fusion.6), channel_id=1, source_target_pairs={{0,2},{2,0},{1,3},{3,1},{4,6},{6,4},{5,7},{7,5},{8,10},{10,8},{9,1... | collective-permute-start | bytes 3145736 | tf_op jit(solution)/shard_map/ppermute | solution.py:28
  5.7 1.8 %fusion.5 = bf16[16,2,128,128]{3,2,1,0:T(8,128)(2,1)S(1)} fusion(f32[16,2,2,128,128]{4,3,2,1,0:T(8,128)} %bitcast.39, s32[]{:T(128)S(6)} %select_n.24), kind=kLoop, calls=%fused_computation.14 | loop fusion | bytes 2097156 | tf_op jit(solution)/shard_map/convert_element_type | solution.py:26
  7.5 0.5 collective-permute-done
  8.0 0.6 fusion.4
  8.6 0.0 copy-start
  8.6 0.0 copy-start.1
  8.7 0.0 copy-start.2
  8.7 0.0 copy-start.3
  8.7 23.6 %all_to_all.10 = bf16[32,128,128]{2,1,0:T(8,128)(2,1)S(1)} all-to-all(bf16[32,128,128]{2,1,0:T(8,128)(2,1)S(1)} %bitcast.34), channel_id=1, replica_groups=mesh['cuts'=4,'x'=4,'y'=4,'core'=2,'dp'=2] {'x','y','dp'}, dimensions={0} | all-to-all | bytes 2097152 | tf_op jit(solution)/shard_map/all_to_all | solution.py:32
  32.3 0.5 fusion.2
  32.8 0.0 copy-done
  32.9 5.2 %collective-permute-start.3 = (bf16[16384]{0:T(1024)(128)(2,1)S(1)}, bf16[16384]{0:T(1024)(128)(2,1)S(1)}, u32[]{:S(2)}, u32[]{:S(2)}) collective-permute-start(bf16[16384]{0:T(1024)(128)(2,1)S(1)} %fusion.12), channel_id=1, source_target_pairs={{0,192},{64,0},{128,64},{192,128},{1,193},{65,1},{129,65},{193,129... | collective-permute-start | bytes 98312 | tf_op jit(solution)/shard_map/ppermute | solution.py:38
  38.1 1.2 %collective-permute-start.2 = (bf16[16384]{0:T(1024)(128)(2,1)S(1)}, bf16[16384]{0:T(1024)(128)(2,1)S(1)}, u32[]{:S(2)}, u32[]{:S(2)}) collective-permute-start(bf16[16384]{0:T(1024)(128)(2,1)S(1)} %fusion.12), channel_id=1, source_target_pairs={{0,128},{64,192},{128,0},{192,64},{1,129},{65,193},{129,1},{193,65... | collective-permute-start | bytes 98312 | tf_op jit(solution)/shard_map/ppermute | solution.py:38
  39.2 2.1 %collective-permute-start.1 = (bf16[16384]{0:T(1024)(128)(2,1)S(1)}, bf16[16384]{0:T(1024)(128)(2,1)S(1)}, u32[]{:S(2)}, u32[]{:S(2)}) collective-permute-start(bf16[16384]{0:T(1024)(128)(2,1)S(1)} %fusion.12), channel_id=1, source_target_pairs={{0,64},{64,128},{128,192},{192,0},{1,65},{65,129},{129,193},{193,1... | collective-permute-start | bytes 98312 | tf_op jit(solution)/shard_map/ppermute | solution.py:38
  41.3 0.7 %multiply_subtract_fusion.1 = f32[1,16384]{1,0:T(1,128)} fusion(f32[1,16384]{1,0:T(1,128)S(1)} %bitcast.37, f32[1,16384]{1,0:T(1,128)S(1)} %copy-done), kind=kLoop, calls=%fused_computation.26 | loop fusion | flops 98304 | bytes 196608 | tf_op jit(solution)/shard_map/sub | solution.py:36
  42.1 0.0 collective-permute-done.3
  42.1 2.7 %collective-permute-done.2 = bf16[16384]{0:T(1024)(128)(2,1)S(1)} collective-permute-done((bf16[16384]{0:T(1024)(128)(2,1)S(1)}, bf16[16384]{0:T(1024)(128)(2,1)S(1)}, u32[]{:S(2)}, u32[]{:S(2)}) %collective-permute-start.2) | collective-permute-done | bytes 32800 | tf_op jit(solution)/shard_map/ppermute | solution.py:38
  44.7 0.0 collective-permute-done.1
  44.7 0.0 copy-done.1
  44.7 0.0 copy-done.2
  44.8 0.0 copy-done.3
  44.8 0.7 %convert_bitcast_fusion = (bf16[128,128]{1,0:T(8,128)(2,1)S(1)}, f32[16384]{0:T(1024)}, f32[16384]{0:T(1024)}, f32[16384]{0:T(1024)}) fusion(f32[16384]{0:T(1024)S(1)} %copy-done.1, f32[16384]{0:T(1024)S(1)} %copy-done.2, f32[16384]{0:T(1024)S(1)} %copy-done.3, bf16[16384]{0:T(1024)(128)(2,1)S(1)} %collective-permute-done.3, ...), kind=kLoop, calls=%fused_computation.27 | loop fusion | flops 442368 | bytes 655360 | tf_op jit(solution)/shard_map/reshape | solution.py:46
  45.5 0.2 broadcast_in_dim.33
  45.7 19.4 %all_to_all.11 = bf16[32,128,128]{2,1,0:T(8,128)(2,1)S(1)} all-to-all(bf16[32,128,128]{2,1,0:T(8,128)(2,1)S(1)} %broadcast_in_dim.33), channel_id=1, replica_groups=mesh['cuts'=4,'x'=4,'y'=4,'core'=2,'dp'=2] {'x','y','dp'}, dimensions={0} | all-to-all | bytes 2097152 | tf_op jit(solution)/shard_map/all_to_all | solution.py:47
  65.2 2.8 %collective-permute-start.4 = (bf16[32,128,128]{2,1,0:T(8,128)(2,1)S(1)}, bf16[32,128,128]{2,1,0:T(8,128)(2,1)S(1)}, u32[]{:S(2)}, u32[]{:S(2)}) collective-permute-start(bf16[32,128,128]{2,1,0:T(8,128)(2,1)S(1)} %all_to_all.11), channel_id=1, source_target_pairs={{0,2},{2,0},{1,3},{3,1},{4,6},{6,4},{5,7},{7,5},{8,10},{10,8},{9,1... | collective-permute-start | bytes 3145736 | tf_op jit(solution)/shard_map/ppermute | solution.py:48
  68.0 2.3 %collective-permute-done.4 = bf16[32,128,128]{2,1,0:T(8,128)(2,1)S(1)} collective-permute-done((bf16[32,128,128]{2,1,0:T(8,128)(2,1)S(1)}, bf16[32,128,128]{2,1,0:T(8,128)(2,1)S(1)}, u32[]{:S(2)}, u32[]{:S(2)}) %collective-permute-start.4) | collective-permute-done | bytes 1048608 | tf_op jit(solution)/shard_map/ppermute | solution.py:48
  70.2 1.5 %broadcast_select_fusion = bf16[16,2,2,128,128]{4,3,2,1,0:T(8,128)(2,1)} fusion(pred[2]{0:T(512)(128)(4,1)S(1)} %iota_compare_fusion, bf16[16,2,128,128]{3,2,1,0:T(8,128)(2,1)S(1)} %bitcast.36, bf16[16,2,128,128]{3,2,1,0:T(8,128)(2,1)S(1)} %bitcast.33), kind=kLoop, calls=%fused_computation.13 | loop fusion | flops 1048576 | bytes 4194306 | tf_op jit(solution)/shard_map/jit(_where)/select_n | solution.py:50
  (2 shorter events, 0.0 us)
Async XLA Ops:
  2.4 5.6 %collective-permute-start = (bf16[16,2,128,128]{3,2,1,0:T(8,128)(2,1)S(1)}, bf16[16,2,128,128]{3,2,1,0:T(8,128)(2,1)S(1)}, u32[]{:S(2)}, u32[]{:S(2)}) collective-permute-start(bf16[16,2,128,128]{3,2,1,0:T(8,128)(2,1)S(1)} %fusion.6), channel_id=1, source_target_pairs={{0,2},{2,0},{1,3},{3,1},{4,6},{6,4},{5,7},{7,5},{8,10},{10,8},{9,1... | collective-permute-start | bytes 3145736 | tf_op jit(solution)/shard_map/ppermute | solution.py:28
  8.6 24.2 %copy-start = (f32[1,16384]{1,0:T(1,128)S(1)}, f32[1,16384]{1,0:T(1,128)}, u32[]{:S(2)}) copy-start(f32[1,16384]{1,0:T(1,128)} %param.6) | copy-start | bytes 196612
  8.6 36.1 %copy-start.1 = (f32[16384]{0:T(1024)S(1)}, f32[16384]{0:T(1024)}, u32[]{:S(2)}) copy-start(f32[16384]{0:T(1024)} %param.7) | copy-start | bytes 196612
  8.7 36.1 %copy-start.2 = (f32[16384]{0:T(1024)S(1)}, f32[16384]{0:T(1024)}, u32[]{:S(2)}) copy-start(f32[16384]{0:T(1024)} %param.8) | copy-start | bytes 196612
  8.7 36.1 %copy-start.3 = (f32[16384]{0:T(1024)S(1)}, f32[16384]{0:T(1024)}, u32[]{:S(2)}) copy-start(f32[16384]{0:T(1024)} %param.9) | copy-start | bytes 196612
  32.9 9.2 %collective-permute-start.3 = (bf16[16384]{0:T(1024)(128)(2,1)S(1)}, bf16[16384]{0:T(1024)(128)(2,1)S(1)}, u32[]{:S(2)}, u32[]{:S(2)}) collective-permute-start(bf16[16384]{0:T(1024)(128)(2,1)S(1)} %fusion.12), channel_id=1, source_target_pairs={{0,192},{64,0},{128,64},{192,128},{1,193},{65,1},{129,65},{193,129... | collective-permute-start | bytes 98312 | tf_op jit(solution)/shard_map/ppermute | solution.py:38
  38.1 6.7 %collective-permute-start.2 = (bf16[16384]{0:T(1024)(128)(2,1)S(1)}, bf16[16384]{0:T(1024)(128)(2,1)S(1)}, u32[]{:S(2)}, u32[]{:S(2)}) collective-permute-start(bf16[16384]{0:T(1024)(128)(2,1)S(1)} %fusion.12), channel_id=1, source_target_pairs={{0,128},{64,192},{128,0},{192,64},{1,129},{65,193},{129,1},{193,65... | collective-permute-start | bytes 98312 | tf_op jit(solution)/shard_map/ppermute | solution.py:38
  39.2 5.5 %collective-permute-start.1 = (bf16[16384]{0:T(1024)(128)(2,1)S(1)}, bf16[16384]{0:T(1024)(128)(2,1)S(1)}, u32[]{:S(2)}, u32[]{:S(2)}) collective-permute-start(bf16[16384]{0:T(1024)(128)(2,1)S(1)} %fusion.12), channel_id=1, source_target_pairs={{0,64},{64,128},{128,192},{192,0},{1,65},{65,129},{129,193},{193,1... | collective-permute-start | bytes 98312 | tf_op jit(solution)/shard_map/ppermute | solution.py:38
  65.2 5.1 %collective-permute-start.4 = (bf16[32,128,128]{2,1,0:T(8,128)(2,1)S(1)}, bf16[32,128,128]{2,1,0:T(8,128)(2,1)S(1)}, u32[]{:S(2)}, u32[]{:S(2)}) collective-permute-start(bf16[32,128,128]{2,1,0:T(8,128)(2,1)S(1)} %all_to_all.11), channel_id=1, source_target_pairs={{0,2},{2,0},{1,3},{3,1},{4,6},{6,4},{5,7},{7,5},{8,10},{10,8},{9,1... | collective-permute-start | bytes 3145736 | tf_op jit(solution)/shard_map/ppermute | solution.py:48

commit v3 on v2

--- a/solution.py
+++ b/solution.py
@@ -1,3 +1,5 @@
+import itertools
+
 import jax
 import jax.numpy as jnp
 from jax import lax
@@ -5,7 +7,6 @@
 
 STEP = 10
 OWN = ("x", "y", "core", "dp")
-CHIPS = ("x", "y", "dp")
 TILE = (128, 128)
 SWAP = [(0, 1), (1, 0)]
 
@@ -20,6 +21,31 @@
     return jnp.where(jnp.abs(code) > 2.0, code * (1.0 / 1024.0) + jnp.clip(code, -1.0, 1.0), code)
 
 
+REDUCE = [(x, y, z) for z, x, y in itertools.product(range(2), range(4), range(4))]
+GATHER = [(x, y, z) for z, x, y in itertools.product(range(2), range(4), range(4))]
+
+
+def exchange(blocks, chips):
+    groups = [
+        [(((cut * 4 + x) * 4 + y) * 2 + core) * 2 + z for x, y, z in (chips[::-1] if core else chips)]
+        for cut in range(4)
+        for core in range(2)
+    ]
+    return lax.all_to_all(blocks, ("cuts",) + OWN, 0, 0, axis_index_groups=groups, tiled=True)
+
+
+def outgoing(own, other, core):
+    code = coded(own.astype(jnp.float32) + other.astype(jnp.float32)).reshape(4, 4, 2, *TILE)
+    code = code.transpose(2, 0, 1, 3, 4)
+    return (jnp.flip(code, (0, 1, 2)) if core else code).reshape(32, *TILE)
+
+
+def in_place(first, second):
+    first, second = first.reshape(2, 4, 4, *TILE), jnp.flip(second.reshape(2, 4, 4, *TILE), (0, 1, 2))
+    first, second = (half.transpose(1, 2, 0, 3, 4).reshape(16, 2, *TILE) for half in (first, second))
+    return jnp.stack([first, second], axis=1)
+
+
 def on_device(grads, residual, master, moment_one, moment_two):
     core = lax.axis_index("core")
     blocks = lax.optimization_barrier(grads.reshape(16, 2, 2, *TILE))
@@ -28,14 +54,15 @@
     other = lax.ppermute(leaving, "core", SWAP)
     blocks, _ = lax.optimization_barrier((blocks, leaving))
     own = lax.optimization_barrier(half(blocks, core))
-    total = own.astype(jnp.float32) + other.astype(jnp.float32)
-    arrived = lax.all_to_all(coded(total).reshape(32, *TILE), CHIPS, 0, 0, tiled=True)
+    zero = core == 0
+    leaving = lax.cond(zero, lambda *halves: outgoing(*halves, 0), lambda *halves: outgoing(*halves, 1), own, other)
+    arrived = exchange(leaving, REDUCE)
     slice_sum = jnp.sum(decoded(arrived), axis=0).reshape(-1)
     corrected = slice_sum + residual[0]
     sent = jnp.floor(corrected * 4.0 + 0.5) * 0.25
     new_residual = (corrected - sent)[None]
     narrow = sent.astype(jnp.bfloat16)
-    sents = [lax.ppermute(narrow, "cuts", [(i, (i + shift) % 4) for i in range(4)]) for shift in (1, 2, 3)]
+    sents = [lax.ppermute(narrow, "cuts", [(i, (i + shift) % 4) for i in range(4)]) for shift in (3, 2, 1)]
     new_residual, sents = lax.optimization_barrier((new_residual, sents))
     gradient = sent + sum(one.astype(jnp.float32) for one in sents)
     new_moment_one = 0.9 * moment_one + 0.1 * gradient
@@ -44,10 +71,9 @@
     second_hat = new_moment_two / (1.0 - 0.95**STEP)
     new_master = master - 0.003 * (first_hat / (jnp.sqrt(second_hat) + 1e-08) + 0.1 * master)
     rounded = new_master.astype(jnp.bfloat16).reshape(TILE)
-    mine = lax.all_to_all(jnp.broadcast_to(rounded, (32, *TILE)), CHIPS, 0, 0, tiled=True)
+    mine = exchange(jnp.broadcast_to(rounded, (32, *TILE)), GATHER)
     theirs = lax.ppermute(mine, "core", SWAP)
-    place = lax.broadcasted_iota(jnp.int32, (1, 2, 1, 1, 1), 1)
-    params = jnp.where(place == core, mine.reshape(16, 1, 2, *TILE), theirs.reshape(16, 1, 2, *TILE))
+    params = in_place(jnp.where(zero, mine, theirs), jnp.where(zero, theirs, mine))
     return (params.reshape(-1), new_master, new_moment_one, new_moment_two, new_residual)
 
 

time: 72 us -> 70 us (0.972)
  blocking collectives: 43.1 us -> 39.5 us
  starting transfers between devices: 14.6 us -> 16.4 us
  local copies, waits for them, and re-layouts: 3.76 us -> 5.53 us
  other arithmetic: 4.17 us -> 2.97 us
  waiting for transfers between devices: 5.49 us -> 4.65 us
    all_to_all x2, blocking collectives: 43.1 us -> 39.5 us  [exchange(): lax.all_to_all(blocks, ('cuts',) + OWN, 0, 0, axis_index_groups=groups, t...]
    ppermute x3, starting transfers between devices: 8.45 us -> 9.99 us  [on_device(): lax.ppermute(narrow, 'cuts', [(i, (i + shift) % 4) for i in range(4)])]
    another operation x0 -> x1, local copies, waits for them, and re-layouts: none -> 1.46 us  [in_place(): return jnp.stack([first, second], axis=1)]
    select_n x1, other arithmetic: 1.53 us -> 0.14 us  [on_device(): jnp.where(zero, mine, theirs)]
    ppermute x3, waiting for transfers between devices: 2.68 us -> 1.83 us  [on_device(): lax.ppermute(narrow, 'cuts', [(i, (i + shift) % 4) for i in range(4)])]
  transfers between devices with their start and end apart: 5 -> 5, of which waited for: 3 -> 3; matrix products, arithmetic and copies ran while one was open for 3% -> 4% of each run, Pallas kernels for 0% -> 0%
where the time goes in v3:
time: 70 us; the launch traced here: 69.8 us
  blocking collectives  39.5 us (56%)
  starting transfers between devices  16.4 us (23%)
  local copies, waits for them, and re-layouts  5.53 us (8%)
  waiting for transfers between devices  4.65 us (7%)
  other arithmetic  2.97 us (4%)
  between operations  0.75 us (1%)
    all_to_all x2, blocking collectives, exchange(): lax.all_to_all(blocks, ('cuts',) + OWN, 0, 0, axis_index_groups=groups, t...  39.5 us
    ppermute x3, starting transfers between devices, on_device(): lax.ppermute(narrow, 'cuts', [(i, (i + shift) % 4) for i in range(4)])  9.99 us
    convert_element_type x2, local copies, waits for them, and re-layouts, on_device(): lax.dynamic_index_in_dim(blocks, which, 1, False).astype(jnp.bfloat16)  3.51 us
    ppermute x1, starting transfers between devices, on_device(): other = lax.ppermute(leaving, 'core', SWAP)  3.33 us
    ppermute x1, starting transfers between devices, on_device(): theirs = lax.ppermute(mine, 'core', SWAP)  3.09 us
    ppermute x1, waiting for transfers between devices, on_device(): theirs = lax.ppermute(mine, 'core', SWAP)  2.29 us
    ppermute x3, waiting for transfers between devices, on_device(): lax.ppermute(narrow, 'cuts', [(i, (i + shift) % 4) for i in range(4)])  1.83 us
    another operation x1, local copies, waits for them, and re-layouts, in_place(): return jnp.stack([first, second], axis=1)  1.46 us
  transfers between devices with their start and end apart: 5, of which 3 were waited for; matrix products, arithmetic and copies ran while one was open for 4% of the time, Pallas kernels for 0%

profile of v3, /device:TPU:1, one launch (start us, length us, event | category | flops | bytes accessed | tf_op | source)
XLA Modules:
  0.0 69.8 jit_solution(16027716722706423599)
XLA Ops:
  0.6 1.8 %fusion.7 = bf16[16,2,128,128]{3,2,1,0:T(8,128)(2,1)S(1)} fusion(f32[16,2,2,128,128]{4,3,2,1,0:T(8,128)} %bitcast.54, s32[]{:T(128)S(6)} %select_n.31), kind=kLoop, calls=%fused_computation.19 | loop fusion | bytes 2097156 | tf_op jit(solution)/shard_map/convert_element_type | solution.py:52
  2.4 3.3 %collective-permute-start = (bf16[16,2,128,128]{3,2,1,0:T(8,128)(2,1)S(1)}, bf16[16,2,128,128]{3,2,1,0:T(8,128)(2,1)S(1)}, u32[]{:S(2)}, u32[]{:S(2)}) collective-permute-start(bf16[16,2,128,128]{3,2,1,0:T(8,128)(2,1)S(1)} %fusion.7), channel_id=1, source_target_pairs={{0,2},{2,0},{1,3},{3,1},{4,6},{6,4},{5,7},{7,5},{8,10},{10,8},{9,1... | collective-permute-start | bytes 3145736 | tf_op jit(solution)/shard_map/ppermute | solution.py:54
  5.7 1.8 %fusion.8 = bf16[16,2,128,128]{3,2,1,0:T(8,128)(2,1)S(1)} fusion(f32[16,2,2,128,128]{4,3,2,1,0:T(8,128)} %bitcast.55, s32[]{:T(128)S(6)} %select_n.32), kind=kLoop, calls=%fused_computation.20 | loop fusion | bytes 2097156 | tf_op jit(solution)/shard_map/convert_element_type | solution.py:52
  7.5 0.5 collective-permute-done
  8.0 0.8 %conditional.1 = (bf16[32,128,128]{2,1,0:T(8,128)(2,1)S(1)}) conditional(s32[]{:T(128)} %convert_element_type.51, (bf16[16,2,128,128]{3,2,1,0:T(8,128)(2,1)S(1)}, bf16[16,2,128,128]{3,2,1,0:T(8,128)(2,1)S(1)}) %tuple.17, (bf16[16,2,128,128]{3,2,1,0:T(8,128)(2,1)S(1)}, bf16[16,2,128,128]{3,2,1,0:T(8,128)(2,1)S(1)}) %tuple.17), branch_computations={%region_0.1_spmd, %region_1.2_spmd} | conditional | flops 4718592 | bytes 7340040 | solution.py:58
  8.0 0.6 fusion.1
  8.6 0.1 copy.20
  8.7 0.1 rev.5
  8.9 0.0 copy-start
  8.9 0.0 copy-start.1
  8.9 0.0 copy-start.2
  8.9 0.0 copy-start.3
  8.9 20.6 %all_to_all.10 = bf16[32,128,128]{2,1,0:T(8,128)(2,1)S(1)} all-to-all(bf16[32,128,128]{2,1,0:T(8,128)(2,1)S(1)} %get-tuple-element.36), channel_id=1, replica_groups={{0,4,8,12,16,20,24,28,32,36,40,44,48,52,56,60,1,5,9,13,17,21,25,29,33,3..., dimensions={0} | all-to-all | bytes 2097152 | tf_op jit(solution)/shard_map/all_to_all | solution.py:34
  29.5 0.5 fusion.6
  30.1 0.0 copy-done
  30.1 3.1 %collective-permute-start.3 = (bf16[16384]{0:T(1024)(128)(2,1)S(1)}, bf16[16384]{0:T(1024)(128)(2,1)S(1)}, u32[]{:S(2)}, u32[]{:S(2)}) collective-permute-start(bf16[16384]{0:T(1024)(128)(2,1)S(1)} %fusion.14), channel_id=1, source_target_pairs={{0,64},{64,128},{128,192},{192,0},{1,65},{65,129},{129,193},{193,1... | collective-permute-start | bytes 98312 | tf_op jit(solution)/shard_map/ppermute | solution.py:65
  33.2 4.5 %collective-permute-start.2 = (bf16[16384]{0:T(1024)(128)(2,1)S(1)}, bf16[16384]{0:T(1024)(128)(2,1)S(1)}, u32[]{:S(2)}, u32[]{:S(2)}) collective-permute-start(bf16[16384]{0:T(1024)(128)(2,1)S(1)} %fusion.14), channel_id=1, source_target_pairs={{0,128},{64,192},{128,0},{192,64},{1,129},{65,193},{129,1},{193,65... | collective-permute-start | bytes 98312 | tf_op jit(solution)/shard_map/ppermute | solution.py:65
  37.7 2.4 %collective-permute-start.1 = (bf16[16384]{0:T(1024)(128)(2,1)S(1)}, bf16[16384]{0:T(1024)(128)(2,1)S(1)}, u32[]{:S(2)}, u32[]{:S(2)}) collective-permute-start(bf16[16384]{0:T(1024)(128)(2,1)S(1)} %fusion.14), channel_id=1, source_target_pairs={{0,192},{64,0},{128,64},{192,128},{1,193},{65,1},{129,65},{193,129... | collective-permute-start | bytes 98312 | tf_op jit(solution)/shard_map/ppermute | solution.py:65
  40.1 0.7 %multiply_subtract_fusion.1 = f32[1,16384]{1,0:T(1,128)} fusion(f32[1,16384]{1,0:T(1,128)S(1)} %bitcast.53, f32[1,16384]{1,0:T(1,128)S(1)} %copy-done), kind=kLoop, calls=%fused_computation.33 | loop fusion | flops 98304 | bytes 196608 | tf_op jit(solution)/shard_map/sub | solution.py:63
  40.8 0.0 collective-permute-done.3
  40.8 0.0 collective-permute-done.2
  40.8 1.8 %collective-permute-done.1 = bf16[16384]{0:T(1024)(128)(2,1)S(1)} collective-permute-done((bf16[16384]{0:T(1024)(128)(2,1)S(1)}, bf16[16384]{0:T(1024)(128)(2,1)S(1)}, u32[]{:S(2)}, u32[]{:S(2)}) %collective-permute-start.1) | collective-permute-done | bytes 32800 | tf_op jit(solution)/shard_map/ppermute | solution.py:65
  42.7 0.0 copy-done.1
  42.7 0.7 %convert_bitcast_fusion = (bf16[128,128]{1,0:T(8,128)(2,1)S(1)}, f32[16384]{0:T(1024)}, f32[16384]{0:T(1024)}, f32[16384]{0:T(1024)}) fusion(f32[16384]{0:T(1024)S(1)} %copy-done.1, f32[16384]{0:T(1024)S(1)} %copy-done.2, f32[16384]{0:T(1024)S(1)} %copy-done.3, bf16[16384]{0:T(1024)(128)(2,1)S(1)} %collective-permute-done.3, ...), kind=kLoop, calls=%fused_computation.34 | loop fusion | flops 442368 | bytes 655360 | tf_op jit(solution)/shard_map/reshape | solution.py:73
  43.4 0.2 broadcast_in_dim.4
  43.6 18.9 %all_to_all.11 = bf16[32,128,128]{2,1,0:T(8,128)(2,1)S(1)} all-to-all(bf16[32,128,128]{2,1,0:T(8,128)(2,1)S(1)} %broadcast_in_dim.4), channel_id=1, replica_groups={{0,4,8,12,16,20,24,28,32,36,40,44,48,52,56,60,1,5,9,13,17,21,25,29,33,3..., dimensions={0} | all-to-all | bytes 2097152 | tf_op jit(solution)/shard_map/all_to_all | solution.py:34
  62.5 3.1 %collective-permute-start.4 = (bf16[32,128,128]{2,1,0:T(8,128)(2,1)S(1)}, bf16[32,128,128]{2,1,0:T(8,128)(2,1)S(1)}, u32[]{:S(2)}, u32[]{:S(2)}) collective-permute-start(bf16[32,128,128]{2,1,0:T(8,128)(2,1)S(1)} %all_to_all.11), channel_id=1, source_target_pairs={{0,2},{2,0},{1,3},{3,1},{4,6},{6,4},{5,7},{7,5},{8,10},{10,8},{9,1... | collective-permute-start | bytes 3145736 | tf_op jit(solution)/shard_map/ppermute | solution.py:75
  65.6 2.3 %collective-permute-done.4 = bf16[32,128,128]{2,1,0:T(8,128)(2,1)S(1)} collective-permute-done((bf16[32,128,128]{2,1,0:T(8,128)(2,1)S(1)}, bf16[32,128,128]{2,1,0:T(8,128)(2,1)S(1)}, u32[]{:S(2)}, u32[]{:S(2)}) %collective-permute-start.4) | collective-permute-done | bytes 1048608 | tf_op jit(solution)/shard_map/ppermute | solution.py:75
  67.9 0.1 broadcast_select_fusion.1
  68.0 0.1 rev.7
  68.1 0.2 pad_maximum_fusion
  68.3 1.5 %copy.18 = bf16[16,2,2,128,128]{4,3,2,1,0:T(8,128)(2,1)} copy(bf16[16,2,2,128,128]{4,3,0,2,1:T(8,128)(2,1)S(1)} %pad_maximum_fusion) | data formatting | bytes 4194304 | tf_op jit(solution)/shard_map/stack | solution.py:46
  (3 shorter events, 0.0 us)
Async XLA Ops:
  2.4 5.6 %collective-permute-start = (bf16[16,2,128,128]{3,2,1,0:T(8,128)(2,1)S(1)}, bf16[16,2,128,128]{3,2,1,0:T(8,128)(2,1)S(1)}, u32[]{:S(2)}, u32[]{:S(2)}) collective-permute-start(bf16[16,2,128,128]{3,2,1,0:T(8,128)(2,1)S(1)} %fusion.7), channel_id=1, source_target_pairs={{0,2},{2,0},{1,3},{3,1},{4,6},{6,4},{5,7},{7,5},{8,10},{10,8},{9,1... | collective-permute-start | bytes 3145736 | tf_op jit(solution)/shard_map/ppermute | solution.py:54
  8.9 21.2 %copy-start = (f32[1,16384]{1,0:T(1,128)S(1)}, f32[1,16384]{1,0:T(1,128)}, u32[]{:S(2)}) copy-start(f32[1,16384]{1,0:T(1,128)} %param.8) | copy-start | bytes 196612
  8.9 33.8 %copy-start.1 = (f32[16384]{0:T(1024)S(1)}, f32[16384]{0:T(1024)}, u32[]{:S(2)}) copy-start(f32[16384]{0:T(1024)} %param.9) | copy-start | bytes 196612
  8.9 33.8 %copy-start.2 = (f32[16384]{0:T(1024)S(1)}, f32[16384]{0:T(1024)}, u32[]{:S(2)}) copy-start(f32[16384]{0:T(1024)} %param.10) | copy-start | bytes 196612
  8.9 33.8 %copy-start.3 = (f32[16384]{0:T(1024)S(1)}, f32[16384]{0:T(1024)}, u32[]{:S(2)}) copy-start(f32[16384]{0:T(1024)} %param.11) | copy-start | bytes 196612
  30.1 10.7 %collective-permute-start.3 = (bf16[16384]{0:T(1024)(128)(2,1)S(1)}, bf16[16384]{0:T(1024)(128)(2,1)S(1)}, u32[]{:S(2)}, u32[]{:S(2)}) collective-permute-start(bf16[16384]{0:T(1024)(128)(2,1)S(1)} %fusion.14), channel_id=1, source_target_pairs={{0,64},{64,128},{128,192},{192,0},{1,65},{65,129},{129,193},{193,1... | collective-permute-start | bytes 98312 | tf_op jit(solution)/shard_map/ppermute | solution.py:65
  33.2 7.7 %collective-permute-start.2 = (bf16[16384]{0:T(1024)(128)(2,1)S(1)}, bf16[16384]{0:T(1024)(128)(2,1)S(1)}, u32[]{:S(2)}, u32[]{:S(2)}) collective-permute-start(bf16[16384]{0:T(1024)(128)(2,1)S(1)} %fusion.14), channel_id=1, source_target_pairs={{0,128},{64,192},{128,0},{192,64},{1,129},{65,193},{129,1},{193,65... | collective-permute-start | bytes 98312 | tf_op jit(solution)/shard_map/ppermute | solution.py:65
  37.7 5.0 %collective-permute-start.1 = (bf16[16384]{0:T(1024)(128)(2,1)S(1)}, bf16[16384]{0:T(1024)(128)(2,1)S(1)}, u32[]{:S(2)}, u32[]{:S(2)}) collective-permute-start(bf16[16384]{0:T(1024)(128)(2,1)S(1)} %fusion.14), channel_id=1, source_target_pairs={{0,192},{64,0},{128,64},{192,128},{1,193},{65,1},{129,65},{193,129... | collective-permute-start | bytes 98312 | tf_op jit(solution)/shard_map/ppermute | solution.py:65
  62.5 5.4 %collective-permute-start.4 = (bf16[32,128,128]{2,1,0:T(8,128)(2,1)S(1)}, bf16[32,128,128]{2,1,0:T(8,128)(2,1)S(1)}, u32[]{:S(2)}, u32[]{:S(2)}) collective-permute-start(bf16[32,128,128]{2,1,0:T(8,128)(2,1)S(1)} %all_to_all.11), channel_id=1, source_target_pairs={{0,2},{2,0},{1,3},{3,1},{4,6},{6,4},{5,7},{7,5},{8,10},{10,8},{9,1... | collective-permute-start | bytes 3145736 | tf_op jit(solution)/shard_map/ppermute | solution.py:75

commit v4 on v3

--- a/solution.py
+++ b/solution.py
@@ -21,8 +21,8 @@
     return jnp.where(jnp.abs(code) > 2.0, code * (1.0 / 1024.0) + jnp.clip(code, -1.0, 1.0), code)
 
 
-REDUCE = [(x, y, z) for z, x, y in itertools.product(range(2), range(4), range(4))]
-GATHER = [(x, y, z) for z, x, y in itertools.product(range(2), range(4), range(4))]
+REDUCE = [(x, y, z) for z, y, x in itertools.product(range(2), range(4), range(4))]
+GATHER = [(x, y, z) for z, y, x in itertools.product(range(2), range(4), range(4))]
 
 
 def exchange(blocks, chips):
@@ -36,14 +36,23 @@
 
 def outgoing(own, other, core):
     code = coded(own.astype(jnp.float32) + other.astype(jnp.float32)).reshape(4, 4, 2, *TILE)
-    code = code.transpose(2, 0, 1, 3, 4)
+    code = code.transpose(2, 1, 0, 3, 4)
     return (jnp.flip(code, (0, 1, 2)) if core else code).reshape(32, *TILE)
 
 
 def in_place(first, second):
     first, second = first.reshape(2, 4, 4, *TILE), jnp.flip(second.reshape(2, 4, 4, *TILE), (0, 1, 2))
-    first, second = (half.transpose(1, 2, 0, 3, 4).reshape(16, 2, *TILE) for half in (first, second))
+    first, second = (half.transpose(2, 1, 0, 3, 4).reshape(16, 2, *TILE) for half in (first, second))
     return jnp.stack([first, second], axis=1)
+
+
+def update(gradient, master, moment_one, moment_two):
+    new_moment_one = 0.9 * moment_one + 0.1 * gradient
+    new_moment_two = 0.95 * moment_two + 0.05 * gradient * gradient
+    first_hat = new_moment_one / (1.0 - 0.9**STEP)
+    second_hat = new_moment_two / (1.0 - 0.95**STEP)
+    new_master = master - 0.003 * (first_hat / (jnp.sqrt(second_hat) + 1e-08) + 0.1 * master)
+    return new_master, new_moment_one, new_moment_two
 
 
 def on_device(grads, residual, master, moment_one, moment_two):
@@ -65,14 +74,12 @@
     sents = [lax.ppermute(narrow, "cuts", [(i, (i + shift) % 4) for i in range(4)]) for shift in (3, 2, 1)]
     new_residual, sents = lax.optimization_barrier((new_residual, sents))
     gradient = sent + sum(one.astype(jnp.float32) for one in sents)
-    new_moment_one = 0.9 * moment_one + 0.1 * gradient
-    new_moment_two = 0.95 * moment_two + 0.05 * gradient * gradient
-    first_hat = new_moment_one / (1.0 - 0.9**STEP)
-    second_hat = new_moment_two / (1.0 - 0.95**STEP)
-    new_master = master - 0.003 * (first_hat / (jnp.sqrt(second_hat) + 1e-08) + 0.1 * master)
-    rounded = new_master.astype(jnp.bfloat16).reshape(TILE)
+    state = (gradient, master, moment_one, moment_two)
+    rounded = update(*state)[0].astype(jnp.bfloat16).reshape(TILE)
     mine = exchange(jnp.broadcast_to(rounded, (32, *TILE)), GATHER)
+    mine, state = lax.optimization_barrier((mine, state))
     theirs = lax.ppermute(mine, "core", SWAP)
+    new_master, new_moment_one, new_moment_two = update(*state)
     params = in_place(jnp.where(zero, mine, theirs), jnp.where(zero, theirs, mine))
     return (params.reshape(-1), new_master, new_moment_one, new_moment_two, new_residual)
 

time: 70 us -> 69.7 us (level)
  blocking collectives: 39.5 us -> 38.8 us
    ppermute x3, waiting for transfers between devices: 1.83 us -> 2.77 us  [on_device(): lax.ppermute(narrow, 'cuts', [(i, (i + shift) % 4) for i in range(4)])]
  transfers between devices with their start and end apart: 5 -> 5, of which waited for: 3 -> 3; matrix products, arithmetic and copies ran while one was open for 4% -> 5% of each run, Pallas kernels for 0% -> 0%
where the time goes in v4:
time: 69.7 us; the launch traced here: 69.4 us
  blocking collectives  38.8 us (56%)
  starting transfers between devices  16.2 us (23%)
  local copies, waits for them, and re-layouts  5.64 us (8%)
  waiting for transfers between devices  4.89 us (7%)
  other arithmetic  3.04 us (4%)
  between operations  0.77 us (1%)
    all_to_all x2, blocking collectives, exchange(): lax.all_to_all(blocks, ('cuts',) + OWN, 0, 0, axis_index_groups=groups, t...  38.8 us
    ppermute x3, starting transfers between devices, on_device(): lax.ppermute(narrow, 'cuts', [(i, (i + shift) % 4) for i in range(4)])  9.45 us
    convert_element_type x2, local copies, waits for them, and re-layouts, on_device(): lax.dynamic_index_in_dim(blocks, which, 1, False).astype(jnp.bfloat16)  3.51 us
    ppermute x1, starting transfers between devices, on_device(): theirs = lax.ppermute(mine, 'core', SWAP)  3.46 us
    ppermute x1, starting transfers between devices, on_device(): other = lax.ppermute(leaving, 'core', SWAP)  3.33 us
    ppermute x3, waiting for transfers between devices, on_device(): lax.ppermute(narrow, 'cuts', [(i, (i + shift) % 4) for i in range(4)])  2.77 us
    ppermute x1, waiting for transfers between devices, on_device(): theirs = lax.ppermute(mine, 'core', SWAP)  1.59 us
    another operation x1, local copies, waits for them, and re-layouts, in_place(): return jnp.stack([first, second], axis=1)  1.46 us
  transfers between devices with their start and end apart: 5, of which 3 were waited for; matrix products, arithmetic and copies ran while one was open for 5% of the time, Pallas kernels for 0%

profile of v4, /device:TPU:1, one launch (start us, length us, event | category | flops | bytes accessed | tf_op | source)
XLA Modules:
  0.0 69.4 jit_solution(993361369980040089)
XLA Ops:
  0.6 1.8 %fusion.7 = bf16[16,2,128,128]{3,2,1,0:T(8,128)(2,1)S(1)} fusion(f32[16,2,2,128,128]{4,3,2,1,0:T(8,128)} %bitcast.52, s32[]{:T(128)S(6)} %select_n.31), kind=kLoop, calls=%fused_computation.19 | loop fusion | bytes 2097156 | tf_op jit(solution)/shard_map/convert_element_type | solution.py:61
  2.4 3.3 %collective-permute-start = (bf16[16,2,128,128]{3,2,1,0:T(8,128)(2,1)S(1)}, bf16[16,2,128,128]{3,2,1,0:T(8,128)(2,1)S(1)}, u32[]{:S(2)}, u32[]{:S(2)}) collective-permute-start(bf16[16,2,128,128]{3,2,1,0:T(8,128)(2,1)S(1)} %fusion.7), channel_id=1, source_target_pairs={{0,2},{2,0},{1,3},{3,1},{4,6},{6,4},{5,7},{7,5},{8,10},{10,8},{9,1... | collective-permute-start | bytes 3145736 | tf_op jit(solution)/shard_map/ppermute | solution.py:63
  5.7 1.8 %fusion.8 = bf16[16,2,128,128]{3,2,1,0:T(8,128)(2,1)S(1)} fusion(f32[16,2,2,128,128]{4,3,2,1,0:T(8,128)} %bitcast.53, s32[]{:T(128)S(6)} %select_n.32), kind=kLoop, calls=%fused_computation.20 | loop fusion | bytes 2097156 | tf_op jit(solution)/shard_map/convert_element_type | solution.py:61
  7.5 0.5 collective-permute-done
  8.0 0.8 %conditional.1 = (bf16[32,128,128]{2,1,0:T(8,128)(2,1)S(1)}) conditional(s32[]{:T(128)} %convert_element_type.51, (bf16[16,2,128,128]{3,2,1,0:T(8,128)(2,1)S(1)}, bf16[16,2,128,128]{3,2,1,0:T(8,128)(2,1)S(1)}) %tuple.18, (bf16[16,2,128,128]{3,2,1,0:T(8,128)(2,1)S(1)}, bf16[16,2,128,128]{3,2,1,0:T(8,128)(2,1)S(1)}) %tuple.18), branch_computations={%region_0.1_spmd, %region_1.2_spmd} | conditional | flops 4718592 | bytes 7340040 | solution.py:67
  8.0 0.6 fusion.1
  8.6 0.1 copy.20
  8.7 0.1 rev.5
  8.9 0.0 copy-start
  8.9 0.0 copy-start.1
  8.9 0.0 copy-start.2
  8.9 0.0 copy-start.3
  8.9 19.8 %all_to_all.10 = bf16[32,128,128]{2,1,0:T(8,128)(2,1)S(1)} all-to-all(bf16[32,128,128]{2,1,0:T(8,128)(2,1)S(1)} %get-tuple-element.47), channel_id=1, replica_groups={{0,16,32,48,4,20,36,52,8,24,40,56,12,28,44,60,1,17,33,49,5,21,37,53,9,2..., dimensions={0} | all-to-all | bytes 2097152 | tf_op jit(solution)/shard_map/all_to_all | solution.py:34
  28.7 0.5 fusion.6
  29.3 6.2 %collective-permute-start.1 = (bf16[16384]{0:T(1024)(128)(2,1)S(1)}, bf16[16384]{0:T(1024)(128)(2,1)S(1)}, u32[]{:S(2)}, u32[]{:S(2)}) collective-permute-start(bf16[16384]{0:T(1024)(128)(2,1)S(1)} %fusion.21), channel_id=1, source_target_pairs={{0,192},{64,0},{128,64},{192,128},{1,193},{65,1},{129,65},{193,129... | collective-permute-start | bytes 98312 | tf_op jit(solution)/shard_map/ppermute | solution.py:74
  35.5 1.0 %collective-permute-start.2 = (bf16[16384]{0:T(1024)(128)(2,1)S(1)}, bf16[16384]{0:T(1024)(128)(2,1)S(1)}, u32[]{:S(2)}, u32[]{:S(2)}) collective-permute-start(bf16[16384]{0:T(1024)(128)(2,1)S(1)} %fusion.21), channel_id=1, source_target_pairs={{0,128},{64,192},{128,0},{192,64},{1,129},{65,193},{129,1},{193,65... | collective-permute-start | bytes 98312 | tf_op jit(solution)/shard_map/ppermute | solution.py:74
  36.5 2.3 %collective-permute-start.3 = (bf16[16384]{0:T(1024)(128)(2,1)S(1)}, bf16[16384]{0:T(1024)(128)(2,1)S(1)}, u32[]{:S(2)}, u32[]{:S(2)}) collective-permute-start(bf16[16384]{0:T(1024)(128)(2,1)S(1)} %fusion.21), channel_id=1, source_target_pairs={{0,64},{64,128},{128,192},{192,0},{1,65},{65,129},{129,193},{193,1... | collective-permute-start | bytes 98312 | tf_op jit(solution)/shard_map/ppermute | solution.py:74
  38.8 0.7 %multiply_subtract_fusion.1 = f32[1,16384]{1,0:T(1,128)} fusion(f32[1,16384]{1,0:T(1,128)S(1)} %bitcast.54, f32[1,16384]{1,0:T(1,128)S(1)} %copy-done), kind=kLoop, calls=%fused_computation.42 | loop fusion | flops 98304 | bytes 196608 | tf_op jit(solution)/shard_map/sub | solution.py:72
  39.5 2.8 %collective-permute-done.2 = bf16[16384]{0:T(1024)(128)(2,1)S(1)} collective-permute-done((bf16[16384]{0:T(1024)(128)(2,1)S(1)}, bf16[16384]{0:T(1024)(128)(2,1)S(1)}, u32[]{:S(2)}, u32[]{:S(2)}) %collective-permute-start.2) | collective-permute-done | bytes 32800 | tf_op jit(solution)/shard_map/ppermute | solution.py:74
  42.3 0.0 collective-permute-done.3
  42.3 0.1 fusion.20
  42.4 0.2 broadcast_in_dim.4
  42.6 19.0 %all_to_all.11 = bf16[32,128,128]{2,1,0:T(8,128)(2,1)S(1)} all-to-all(bf16[32,128,128]{2,1,0:T(8,128)(2,1)S(1)} %broadcast_in_dim.4), channel_id=1, replica_groups={{0,16,32,48,4,20,36,52,8,24,40,56,12,28,44,60,1,17,33,49,5,21,37,53,9,2..., dimensions={0} | all-to-all | bytes 2097152 | tf_op jit(solution)/shard_map/all_to_all | solution.py:34
  61.6 3.5 %collective-permute-start.4 = (bf16[32,128,128]{2,1,0:T(8,128)(2,1)S(1)}, bf16[32,128,128]{2,1,0:T(8,128)(2,1)S(1)}, u32[]{:S(2)}, u32[]{:S(2)}) collective-permute-start(bf16[32,128,128]{2,1,0:T(8,128)(2,1)S(1)} %all_to_all.11), channel_id=1, source_target_pairs={{0,2},{2,0},{1,3},{3,1},{4,6},{6,4},{5,7},{7,5},{8,10},{10,8},{9,1... | collective-permute-start | bytes 3145736 | tf_op jit(solution)/shard_map/ppermute | solution.py:81
  65.1 0.7 %multiply_subtract_fusion = (f32[16384]{0:T(1024)}, f32[16384]{0:T(1024)}, f32[16384]{0:T(1024)}) fusion(f32[16384]{0:T(1024)S(1)} %copy-done.1, f32[16384]{0:T(1024)S(1)} %get-tuple-element.37, f32[16384]{0:T(1024)S(1)} %copy-done.3, f32[16384]{0:T(1024)S(1)} %copy-done.2), kind=kLoop, calls=%fused_computation.38 | loop fusion | flops 245760 | bytes 458752 | tf_op jit(solution)/shard_map/sub | solution.py:54
  65.8 1.6 %collective-permute-done.4 = bf16[32,128,128]{2,1,0:T(8,128)(2,1)S(1)} collective-permute-done((bf16[32,128,128]{2,1,0:T(8,128)(2,1)S(1)}, bf16[32,128,128]{2,1,0:T(8,128)(2,1)S(1)}, u32[]{:S(2)}, u32[]{:S(2)}) %collective-permute-start.4) | collective-permute-done | bytes 1048608 | tf_op jit(solution)/shard_map/ppermute | solution.py:81
  67.4 0.1 broadcast_select_fusion.1
  67.5 0.1 reverse_bitcast_fusion
  67.6 0.1 copy.17
  67.7 0.1 copy.16
  67.8 0.2 pad_maximum_fusion
  68.0 1.5 %copy.18 = bf16[16,2,2,128,128]{4,3,2,1,0:T(8,128)(2,1)} copy(bf16[16,2,2,128,128]{4,3,2,0,1:T(8,128)(2,1)S(1)} %pad_maximum_fusion) | data formatting | bytes 4194304 | tf_op jit(solution)/shard_map/stack | solution.py:46
  (6 shorter events, 0.0 us)
Async XLA Ops:
  2.4 5.6 %collective-permute-start = (bf16[16,2,128,128]{3,2,1,0:T(8,128)(2,1)S(1)}, bf16[16,2,128,128]{3,2,1,0:T(8,128)(2,1)S(1)}, u32[]{:S(2)}, u32[]{:S(2)}) collective-permute-start(bf16[16,2,128,128]{3,2,1,0:T(8,128)(2,1)S(1)} %fusion.7), channel_id=1, source_target_pairs={{0,2},{2,0},{1,3},{3,1},{4,6},{6,4},{5,7},{7,5},{8,10},{10,8},{9,1... | collective-permute-start | bytes 3145736 | tf_op jit(solution)/shard_map/ppermute | solution.py:63
  8.9 20.4 %copy-start = (f32[1,16384]{1,0:T(1,128)S(1)}, f32[1,16384]{1,0:T(1,128)}, u32[]{:S(2)}) copy-start(f32[1,16384]{1,0:T(1,128)} %param.8) | copy-start | bytes 196612
  8.9 33.4 %copy-start.1 = (f32[16384]{0:T(1024)S(1)}, f32[16384]{0:T(1024)}, u32[]{:S(2)}) copy-start(f32[16384]{0:T(1024)} %param.9) | copy-start | bytes 196612
  8.9 33.4 %copy-start.2 = (f32[16384]{0:T(1024)S(1)}, f32[16384]{0:T(1024)}, u32[]{:S(2)}) copy-start(f32[16384]{0:T(1024)} %param.11) | copy-start | bytes 196612
  8.9 33.4 %copy-start.3 = (f32[16384]{0:T(1024)S(1)}, f32[16384]{0:T(1024)}, u32[]{:S(2)}) copy-start(f32[16384]{0:T(1024)} %param.10) | copy-start | bytes 196612
  29.3 10.2 %collective-permute-start.1 = (bf16[16384]{0:T(1024)(128)(2,1)S(1)}, bf16[16384]{0:T(1024)(128)(2,1)S(1)}, u32[]{:S(2)}, u32[]{:S(2)}) collective-permute-start(bf16[16384]{0:T(1024)(128)(2,1)S(1)} %fusion.21), channel_id=1, source_target_pairs={{0,192},{64,0},{128,64},{192,128},{1,193},{65,1},{129,65},{193,129... | collective-permute-start | bytes 98312 | tf_op jit(solution)/shard_map/ppermute | solution.py:74
  35.5 6.8 %collective-permute-start.2 = (bf16[16384]{0:T(1024)(128)(2,1)S(1)}, bf16[16384]{0:T(1024)(128)(2,1)S(1)}, u32[]{:S(2)}, u32[]{:S(2)}) collective-permute-start(bf16[16384]{0:T(1024)(128)(2,1)S(1)} %fusion.21), channel_id=1, source_target_pairs={{0,128},{64,192},{128,0},{192,64},{1,129},{65,193},{129,1},{193,65... | collective-permute-start | bytes 98312 | tf_op jit(solution)/shard_map/ppermute | solution.py:74
  36.5 5.8 %collective-permute-start.3 = (bf16[16384]{0:T(1024)(128)(2,1)S(1)}, bf16[16384]{0:T(1024)(128)(2,1)S(1)}, u32[]{:S(2)}, u32[]{:S(2)}) collective-permute-start(bf16[16384]{0:T(1024)(128)(2,1)S(1)} %fusion.21), channel_id=1, source_target_pairs={{0,64},{64,128},{128,192},{192,0},{1,65},{65,129},{129,193},{193,1... | collective-permute-start | bytes 98312 | tf_op jit(solution)/shard_map/ppermute | solution.py:74
  61.6 5.7 %collective-permute-start.4 = (bf16[32,128,128]{2,1,0:T(8,128)(2,1)S(1)}, bf16[32,128,128]{2,1,0:T(8,128)(2,1)S(1)}, u32[]{:S(2)}, u32[]{:S(2)}) collective-permute-start(bf16[32,128,128]{2,1,0:T(8,128)(2,1)S(1)} %all_to_all.11), channel_id=1, source_target_pairs={{0,2},{2,0},{1,3},{3,1},{4,6},{6,4},{5,7},{7,5},{8,10},{10,8},{9,1... | collective-permute-start | bytes 3145736 | tf_op jit(solution)/shard_map/ppermute | solution.py:81

commit v5 on v4

--- a/solution.py
+++ b/solution.py
@@ -9,6 +9,10 @@
 OWN = ("x", "y", "core", "dp")
 TILE = (128, 128)
 SWAP = [(0, 1), (1, 0)]
+TURNS = [
+    [(2 * cut + core, 2 * ((cut + (-shift if core else shift)) % 4) + core) for cut in range(4) for core in range(2)]
+    for shift in (3, 2, 1)
+]
 
 
 def coded(total):
@@ -71,7 +75,7 @@
     sent = jnp.floor(corrected * 4.0 + 0.5) * 0.25
     new_residual = (corrected - sent)[None]
     narrow = sent.astype(jnp.bfloat16)
-    sents = [lax.ppermute(narrow, "cuts", [(i, (i + shift) % 4) for i in range(4)]) for shift in (3, 2, 1)]
+    sents = [lax.ppermute(narrow, ("cuts", "core"), turn) for turn in TURNS]
     new_residual, sents = lax.optimization_barrier((new_residual, sents))
     gradient = sent + sum(one.astype(jnp.float32) for one in sents)
     state = (gradient, master, moment_one, moment_two)

time: 69.7 us -> 68.9 us (0.989)
  starting transfers between devices: 16.2 us -> 18.5 us
  waiting for transfers between devices: 4.89 us -> 2.66 us
  blocking collectives: 38.8 us -> 38 us
    ppermute x3, waiting for transfers between devices: 2.77 us -> 0.54 us  [on_device(): sents = [lax.ppermute(narrow, ('cuts', 'core'), turn) for turn in TURNS]]
    ppermute x3, starting transfers between devices: 9.45 us -> 10.7 us  [on_device(): sents = [lax.ppermute(narrow, ('cuts', 'core'), turn) for turn in TURNS]]
    ppermute x1, starting transfers between devices: 3.46 us -> 4.47 us  [on_device(): theirs = lax.ppermute(mine, 'core', SWAP)]
    all_to_all x2, blocking collectives: 38.8 us -> 38 us  [exchange(): lax.all_to_all(blocks, ('cuts',) + OWN, 0, 0, axis_index_groups=groups, t...]
where the time goes in v5:
time: 68.9 us; the launch traced here: 68.6 us
  blocking collectives  38 us (55%)
  starting transfers between devices  18.5 us (27%)
  local copies, waits for them, and re-layouts  5.64 us (8%)
  other arithmetic  3.04 us (4%)
  waiting for transfers between devices  2.66 us (4%)
  between operations  0.76 us (1%)
    all_to_all x2, blocking collectives, exchange(): lax.all_to_all(blocks, ('cuts',) + OWN, 0, 0, axis_index_groups=groups, t...  38 us
    ppermute x3, starting transfers between devices, on_device(): sents = [lax.ppermute(narrow, ('cuts', 'core'), turn) for turn in TURNS]  10.7 us
    ppermute x1, starting transfers between devices, on_device(): theirs = lax.ppermute(mine, 'core', SWAP)  4.47 us
    convert_element_type x2, local copies, waits for them, and re-layouts, on_device(): lax.dynamic_index_in_dim(blocks, which, 1, False).astype(jnp.bfloat16)  3.51 us
    ppermute x1, starting transfers between devices, on_device(): other = lax.ppermute(leaving, 'core', SWAP)  3.33 us
    ppermute x1, waiting for transfers between devices, on_device(): theirs = lax.ppermute(mine, 'core', SWAP)  1.59 us
    another operation x1, local copies, waits for them, and re-layouts, in_place(): return jnp.stack([first, second], axis=1)  1.46 us
  transfers between devices with their start and end apart: 5, of which 3 were waited for; matrix products, arithmetic and copies ran while one was open for 5% of the time, Pallas kernels for 0%

profile of v5, /device:TPU:1, one launch (start us, length us, event | category | flops | bytes accessed | tf_op | source)
XLA Modules:
  0.0 68.6 jit_solution(18253112125319401225)
XLA Ops:
  0.6 1.8 %fusion.7 = bf16[16,2,128,128]{3,2,1,0:T(8,128)(2,1)S(1)} fusion(f32[16,2,2,128,128]{4,3,2,1,0:T(8,128)} %bitcast.52, s32[]{:T(128)S(6)} %select_n.31), kind=kLoop, calls=%fused_computation.19 | loop fusion | bytes 2097156 | tf_op jit(solution)/shard_map/convert_element_type | solution.py:65
  2.4 3.3 %collective-permute-start = (bf16[16,2,128,128]{3,2,1,0:T(8,128)(2,1)S(1)}, bf16[16,2,128,128]{3,2,1,0:T(8,128)(2,1)S(1)}, u32[]{:S(2)}, u32[]{:S(2)}) collective-permute-start(bf16[16,2,128,128]{3,2,1,0:T(8,128)(2,1)S(1)} %fusion.7), channel_id=1, source_target_pairs={{0,2},{2,0},{1,3},{3,1},{4,6},{6,4},{5,7},{7,5},{8,10},{10,8},{9,1... | collective-permute-start | bytes 3145736 | tf_op jit(solution)/shard_map/ppermute | solution.py:67
  5.7 1.8 %fusion.8 = bf16[16,2,128,128]{3,2,1,0:T(8,128)(2,1)S(1)} fusion(f32[16,2,2,128,128]{4,3,2,1,0:T(8,128)} %bitcast.53, s32[]{:T(128)S(6)} %select_n.32), kind=kLoop, calls=%fused_computation.20 | loop fusion | bytes 2097156 | tf_op jit(solution)/shard_map/convert_element_type | solution.py:65
  7.5 0.5 collective-permute-done
  8.0 0.8 %conditional.1 = (bf16[32,128,128]{2,1,0:T(8,128)(2,1)S(1)}) conditional(s32[]{:T(128)} %convert_element_type.51, (bf16[16,2,128,128]{3,2,1,0:T(8,128)(2,1)S(1)}, bf16[16,2,128,128]{3,2,1,0:T(8,128)(2,1)S(1)}) %tuple.18, (bf16[16,2,128,128]{3,2,1,0:T(8,128)(2,1)S(1)}, bf16[16,2,128,128]{3,2,1,0:T(8,128)(2,1)S(1)}) %tuple.18), branch_computations={%region_0.1_spmd, %region_1.2_spmd} | conditional | flops 4718592 | bytes 7340040 | solution.py:71
  8.0 0.6 fusion.1
  8.6 0.1 copy.20
  8.7 0.1 rev.5
  8.9 0.0 copy-start
  8.9 0.0 copy-start.1
  8.9 0.0 copy-start.2
  8.9 0.0 copy-start.3
  8.9 19.8 %all_to_all.10 = bf16[32,128,128]{2,1,0:T(8,128)(2,1)S(1)} all-to-all(bf16[32,128,128]{2,1,0:T(8,128)(2,1)S(1)} %get-tuple-element.47), channel_id=1, replica_groups={{0,16,32,48,4,20,36,52,8,24,40,56,12,28,44,60,1,17,33,49,5,21,37,53,9,2..., dimensions={0} | all-to-all | bytes 2097152 | tf_op jit(solution)/shard_map/all_to_all | solution.py:38
  28.7 0.5 fusion.6
  29.3 3.1 %collective-permute-start.1 = (bf16[16384]{0:T(1024)(128)(2,1)S(1)}, bf16[16384]{0:T(1024)(128)(2,1)S(1)}, u32[]{:S(2)}, u32[]{:S(2)}) collective-permute-start(bf16[16384]{0:T(1024)(128)(2,1)S(1)} %fusion.21), channel_id=1, source_target_pairs={{0,192},{2,66},{64,0},{66,130},{128,64},{130,194},{192,128},{194,2... | collective-permute-start | bytes 98312 | tf_op jit(solution)/shard_map/ppermute | solution.py:78
  32.4 5.2 %collective-permute-start.2 = (bf16[16384]{0:T(1024)(128)(2,1)S(1)}, bf16[16384]{0:T(1024)(128)(2,1)S(1)}, u32[]{:S(2)}, u32[]{:S(2)}) collective-permute-start(bf16[16384]{0:T(1024)(128)(2,1)S(1)} %fusion.21), channel_id=1, source_target_pairs={{0,128},{2,130},{64,192},{66,194},{128,0},{130,2},{192,64},{194,66... | collective-permute-start | bytes 98312 | tf_op jit(solution)/shard_map/ppermute | solution.py:78
  37.6 2.4 %collective-permute-start.3 = (bf16[16384]{0:T(1024)(128)(2,1)S(1)}, bf16[16384]{0:T(1024)(128)(2,1)S(1)}, u32[]{:S(2)}, u32[]{:S(2)}) collective-permute-start(bf16[16384]{0:T(1024)(128)(2,1)S(1)} %fusion.21), channel_id=1, source_target_pairs={{0,64},{2,194},{64,128},{66,2},{128,192},{130,66},{192,0},{194,130... | collective-permute-start | bytes 98312 | tf_op jit(solution)/shard_map/ppermute | solution.py:78
  40.0 0.7 %multiply_subtract_fusion.1 = f32[1,16384]{1,0:T(1,128)} fusion(f32[1,16384]{1,0:T(1,128)S(1)} %bitcast.54, f32[1,16384]{1,0:T(1,128)S(1)} %copy-done), kind=kLoop, calls=%fused_computation.42 | loop fusion | flops 98304 | bytes 196608 | tf_op jit(solution)/shard_map/sub | solution.py:76
  40.7 0.0 collective-permute-done.1
  40.7 0.5 collective-permute-done.3
  41.3 0.1 fusion.20
  41.4 0.2 broadcast_in_dim.4
  41.6 18.2 %all_to_all.11 = bf16[32,128,128]{2,1,0:T(8,128)(2,1)S(1)} all-to-all(bf16[32,128,128]{2,1,0:T(8,128)(2,1)S(1)} %broadcast_in_dim.4), channel_id=1, replica_groups={{0,16,32,48,4,20,36,52,8,24,40,56,12,28,44,60,1,17,33,49,5,21,37,53,9,2..., dimensions={0} | all-to-all | bytes 2097152 | tf_op jit(solution)/shard_map/all_to_all | solution.py:38
  59.8 4.5 %collective-permute-start.4 = (bf16[32,128,128]{2,1,0:T(8,128)(2,1)S(1)}, bf16[32,128,128]{2,1,0:T(8,128)(2,1)S(1)}, u32[]{:S(2)}, u32[]{:S(2)}) collective-permute-start(bf16[32,128,128]{2,1,0:T(8,128)(2,1)S(1)} %all_to_all.11), channel_id=1, source_target_pairs={{0,2},{2,0},{1,3},{3,1},{4,6},{6,4},{5,7},{7,5},{8,10},{10,8},{9,1... | collective-permute-start | bytes 3145736 | tf_op jit(solution)/shard_map/ppermute | solution.py:85
  64.3 0.7 %multiply_subtract_fusion = (f32[16384]{0:T(1024)}, f32[16384]{0:T(1024)}, f32[16384]{0:T(1024)}) fusion(f32[16384]{0:T(1024)S(1)} %copy-done.1, f32[16384]{0:T(1024)S(1)} %get-tuple-element.37, f32[16384]{0:T(1024)S(1)} %copy-done.3, f32[16384]{0:T(1024)S(1)} %copy-done.2), kind=kLoop, calls=%fused_computation.38 | loop fusion | flops 245760 | bytes 458752 | tf_op jit(solution)/shard_map/sub | solution.py:58
  65.0 1.6 %collective-permute-done.4 = bf16[32,128,128]{2,1,0:T(8,128)(2,1)S(1)} collective-permute-done((bf16[32,128,128]{2,1,0:T(8,128)(2,1)S(1)}, bf16[32,128,128]{2,1,0:T(8,128)(2,1)S(1)}, u32[]{:S(2)}, u32[]{:S(2)}) %collective-permute-start.4) | collective-permute-done | bytes 1048608 | tf_op jit(solution)/shard_map/ppermute | solution.py:85
  66.6 0.1 broadcast_select_fusion.1
  66.7 0.1 reverse_bitcast_fusion
  66.8 0.1 copy.17
  66.9 0.1 copy.16
  66.9 0.2 pad_maximum_fusion
  67.2 1.5 %copy.18 = bf16[16,2,2,128,128]{4,3,2,1,0:T(8,128)(2,1)} copy(bf16[16,2,2,128,128]{4,3,2,0,1:T(8,128)(2,1)S(1)} %pad_maximum_fusion) | data formatting | bytes 4194304 | tf_op jit(solution)/shard_map/stack | solution.py:50
  (6 shorter events, 0.0 us)
Async XLA Ops:
  2.4 5.6 %collective-permute-start = (bf16[16,2,128,128]{3,2,1,0:T(8,128)(2,1)S(1)}, bf16[16,2,128,128]{3,2,1,0:T(8,128)(2,1)S(1)}, u32[]{:S(2)}, u32[]{:S(2)}) collective-permute-start(bf16[16,2,128,128]{3,2,1,0:T(8,128)(2,1)S(1)} %fusion.7), channel_id=1, source_target_pairs={{0,2},{2,0},{1,3},{3,1},{4,6},{6,4},{5,7},{7,5},{8,10},{10,8},{9,1... | collective-permute-start | bytes 3145736 | tf_op jit(solution)/shard_map/ppermute | solution.py:67
  8.9 20.4 %copy-start = (f32[1,16384]{1,0:T(1,128)S(1)}, f32[1,16384]{1,0:T(1,128)}, u32[]{:S(2)}) copy-start(f32[1,16384]{1,0:T(1,128)} %param.8) | copy-start | bytes 196612
  8.9 32.4 %copy-start.1 = (f32[16384]{0:T(1024)S(1)}, f32[16384]{0:T(1024)}, u32[]{:S(2)}) copy-start(f32[16384]{0:T(1024)} %param.9) | copy-start | bytes 196612
  8.9 32.4 %copy-start.2 = (f32[16384]{0:T(1024)S(1)}, f32[16384]{0:T(1024)}, u32[]{:S(2)}) copy-start(f32[16384]{0:T(1024)} %param.11) | copy-start | bytes 196612
  8.9 32.4 %copy-start.3 = (f32[16384]{0:T(1024)S(1)}, f32[16384]{0:T(1024)}, u32[]{:S(2)}) copy-start(f32[16384]{0:T(1024)} %param.10) | copy-start | bytes 196612
  29.3 11.4 %collective-permute-start.1 = (bf16[16384]{0:T(1024)(128)(2,1)S(1)}, bf16[16384]{0:T(1024)(128)(2,1)S(1)}, u32[]{:S(2)}, u32[]{:S(2)}) collective-permute-start(bf16[16384]{0:T(1024)(128)(2,1)S(1)} %fusion.21), channel_id=1, source_target_pairs={{0,192},{2,66},{64,0},{66,130},{128,64},{130,194},{192,128},{194,2... | collective-permute-start | bytes 98312 | tf_op jit(solution)/shard_map/ppermute | solution.py:78
  32.4 8.3 %collective-permute-start.2 = (bf16[16384]{0:T(1024)(128)(2,1)S(1)}, bf16[16384]{0:T(1024)(128)(2,1)S(1)}, u32[]{:S(2)}, u32[]{:S(2)}) collective-permute-start(bf16[16384]{0:T(1024)(128)(2,1)S(1)} %fusion.21), channel_id=1, source_target_pairs={{0,128},{2,130},{64,192},{66,194},{128,0},{130,2},{192,64},{194,66... | collective-permute-start | bytes 98312 | tf_op jit(solution)/shard_map/ppermute | solution.py:78
  37.6 3.7 %collective-permute-start.3 = (bf16[16384]{0:T(1024)(128)(2,1)S(1)}, bf16[16384]{0:T(1024)(128)(2,1)S(1)}, u32[]{:S(2)}, u32[]{:S(2)}) collective-permute-start(bf16[16384]{0:T(1024)(128)(2,1)S(1)} %fusion.21), channel_id=1, source_target_pairs={{0,64},{2,194},{64,128},{66,2},{128,192},{130,66},{192,0},{194,130... | collective-permute-start | bytes 98312 | tf_op jit(solution)/shard_map/ppermute | solution.py:78
  59.8 6.8 %collective-permute-start.4 = (bf16[32,128,128]{2,1,0:T(8,128)(2,1)S(1)}, bf16[32,128,128]{2,1,0:T(8,128)(2,1)S(1)}, u32[]{:S(2)}, u32[]{:S(2)}) collective-permute-start(bf16[32,128,128]{2,1,0:T(8,128)(2,1)S(1)} %all_to_all.11), channel_id=1, source_target_pairs={{0,2},{2,0},{1,3},{3,1},{4,6},{6,4},{5,7},{7,5},{8,10},{10,8},{9,1... | collective-permute-start | bytes 3145736 | tf_op jit(solution)/shard_map/ppermute | solution.py:85

commit v6 on v5

--- a/solution.py
+++ b/solution.py
@@ -11,7 +11,7 @@
 SWAP = [(0, 1), (1, 0)]
 TURNS = [
     [(2 * cut + core, 2 * ((cut + (-shift if core else shift)) % 4) + core) for cut in range(4) for core in range(2)]
-    for shift in (3, 2, 1)
+    for shift in (2, 1, 3)
 ]
 
 

time: 68.9 us -> 68.9 us (level)
  starting transfers between devices: 18.5 us -> 16.4 us
  waiting for transfers between devices: 2.66 us -> 4.24 us
    ppermute x3, waiting for transfers between devices: 0.54 us -> 2.12 us  [on_device(): sents = [lax.ppermute(narrow, ('cuts', 'core'), turn) for turn in TURNS]]
    ppermute x3, starting transfers between devices: 10.7 us -> 9.45 us  [on_device(): sents = [lax.ppermute(narrow, ('cuts', 'core'), turn) for turn in TURNS]]
    ppermute x1, starting transfers between devices: 4.47 us -> 3.66 us  [on_device(): theirs = lax.ppermute(mine, 'core', SWAP)]
  transfers between devices with their start and end apart: 5 -> 5, of which waited for: 3 -> 4; matrix products, arithmetic and copies ran while one was open for 5% -> 5% of each run, Pallas kernels for 0% -> 0%
where the time goes in v6:
time: 68.9 us; the launch traced here: 68.6 us
  blocking collectives  38.5 us (56%)
  starting transfers between devices  16.4 us (24%)
  local copies, waits for them, and re-layouts  5.64 us (8%)
  waiting for transfers between devices  4.24 us (6%)
  other arithmetic  3.04 us (4%)
  between operations  0.76 us (1%)
    all_to_all x2, blocking collectives, exchange(): lax.all_to_all(blocks, ('cuts',) + OWN, 0, 0, axis_index_groups=groups, t...  38.5 us
    ppermute x3, starting transfers between devices, on_device(): sents = [lax.ppermute(narrow, ('cuts', 'core'), turn) for turn in TURNS]  9.45 us
    ppermute x1, starting transfers between devices, on_device(): theirs = lax.ppermute(mine, 'core', SWAP)  3.66 us
    convert_element_type x2, local copies, waits for them, and re-layouts, on_device(): lax.dynamic_index_in_dim(blocks, which, 1, False).astype(jnp.bfloat16)  3.51 us
    ppermute x1, starting transfers between devices, on_device(): other = lax.ppermute(leaving, 'core', SWAP)  3.33 us
    ppermute x3, waiting for transfers between devices, on_device(): sents = [lax.ppermute(narrow, ('cuts', 'core'), turn) for turn in TURNS]  2.12 us
    ppermute x1, waiting for transfers between devices, on_device(): theirs = lax.ppermute(mine, 'core', SWAP)  1.59 us
    another operation x1, local copies, waits for them, and re-layouts, in_place(): return jnp.stack([first, second], axis=1)  1.46 us
  transfers between devices with their start and end apart: 5, of which 4 were waited for; matrix products, arithmetic and copies ran while one was open for 5% of the time, Pallas kernels for 0%

profile of v6, /device:TPU:1, one launch (start us, length us, event | category | flops | bytes accessed | tf_op | source)
XLA Modules:
  0.0 68.6 jit_solution(11960898915188601566)
XLA Ops:
  0.6 1.8 %fusion.7 = bf16[16,2,128,128]{3,2,1,0:T(8,128)(2,1)S(1)} fusion(f32[16,2,2,128,128]{4,3,2,1,0:T(8,128)} %bitcast.52, s32[]{:T(128)S(6)} %select_n.31), kind=kLoop, calls=%fused_computation.19 | loop fusion | bytes 2097156 | tf_op jit(solution)/shard_map/convert_element_type | solution.py:65
  2.4 3.3 %collective-permute-start = (bf16[16,2,128,128]{3,2,1,0:T(8,128)(2,1)S(1)}, bf16[16,2,128,128]{3,2,1,0:T(8,128)(2,1)S(1)}, u32[]{:S(2)}, u32[]{:S(2)}) collective-permute-start(bf16[16,2,128,128]{3,2,1,0:T(8,128)(2,1)S(1)} %fusion.7), channel_id=1, source_target_pairs={{0,2},{2,0},{1,3},{3,1},{4,6},{6,4},{5,7},{7,5},{8,10},{10,8},{9,1... | collective-permute-start | bytes 3145736 | tf_op jit(solution)/shard_map/ppermute | solution.py:67
  5.7 1.8 %fusion.8 = bf16[16,2,128,128]{3,2,1,0:T(8,128)(2,1)S(1)} fusion(f32[16,2,2,128,128]{4,3,2,1,0:T(8,128)} %bitcast.53, s32[]{:T(128)S(6)} %select_n.32), kind=kLoop, calls=%fused_computation.20 | loop fusion | bytes 2097156 | tf_op jit(solution)/shard_map/convert_element_type | solution.py:65
  7.5 0.5 collective-permute-done
  8.0 0.8 %conditional.1 = (bf16[32,128,128]{2,1,0:T(8,128)(2,1)S(1)}) conditional(s32[]{:T(128)} %convert_element_type.51, (bf16[16,2,128,128]{3,2,1,0:T(8,128)(2,1)S(1)}, bf16[16,2,128,128]{3,2,1,0:T(8,128)(2,1)S(1)}) %tuple.18, (bf16[16,2,128,128]{3,2,1,0:T(8,128)(2,1)S(1)}, bf16[16,2,128,128]{3,2,1,0:T(8,128)(2,1)S(1)}) %tuple.18), branch_computations={%region_0.1_spmd, %region_1.2_spmd} | conditional | flops 4718592 | bytes 7340040 | solution.py:71
  8.0 0.6 fusion.1
  8.6 0.1 copy.20
  8.7 0.1 rev.5
  8.9 0.0 copy-start
  8.9 0.0 copy-start.1
  8.9 0.0 copy-start.2
  8.9 0.0 copy-start.3
  8.9 19.8 %all_to_all.10 = bf16[32,128,128]{2,1,0:T(8,128)(2,1)S(1)} all-to-all(bf16[32,128,128]{2,1,0:T(8,128)(2,1)S(1)} %get-tuple-element.47), channel_id=1, replica_groups={{0,16,32,48,4,20,36,52,8,24,40,56,12,28,44,60,1,17,33,49,5,21,37,53,9,2..., dimensions={0} | all-to-all | bytes 2097152 | tf_op jit(solution)/shard_map/all_to_all | solution.py:38
  28.7 0.5 fusion.6
  29.3 7.1 %collective-permute-start.1 = (bf16[16384]{0:T(1024)(128)(2,1)S(1)}, bf16[16384]{0:T(1024)(128)(2,1)S(1)}, u32[]{:S(2)}, u32[]{:S(2)}) collective-permute-start(bf16[16384]{0:T(1024)(128)(2,1)S(1)} %fusion.21), channel_id=1, source_target_pairs={{0,128},{2,130},{64,192},{66,194},{128,0},{130,2},{192,64},{194,66... | collective-permute-start | bytes 98312 | tf_op jit(solution)/shard_map/ppermute | solution.py:78
  36.4 0.0 collective-permute-start.2
  36.4 2.4 %collective-permute-start.3 = (bf16[16384]{0:T(1024)(128)(2,1)S(1)}, bf16[16384]{0:T(1024)(128)(2,1)S(1)}, u32[]{:S(2)}, u32[]{:S(2)}) collective-permute-start(bf16[16384]{0:T(1024)(128)(2,1)S(1)} %fusion.21), channel_id=1, source_target_pairs={{0,192},{2,66},{64,0},{66,130},{128,64},{130,194},{192,128},{194,2... | collective-permute-start | bytes 98312 | tf_op jit(solution)/shard_map/ppermute | solution.py:78
  38.8 0.7 %multiply_subtract_fusion.1 = f32[1,16384]{1,0:T(1,128)} fusion(f32[1,16384]{1,0:T(1,128)S(1)} %bitcast.54, f32[1,16384]{1,0:T(1,128)S(1)} %copy-done), kind=kLoop, calls=%fused_computation.42 | loop fusion | flops 98304 | bytes 196608 | tf_op jit(solution)/shard_map/sub | solution.py:76
  39.5 0.6 collective-permute-done.2
  40.1 1.6 %collective-permute-done.3 = bf16[16384]{0:T(1024)(128)(2,1)S(1)} collective-permute-done((bf16[16384]{0:T(1024)(128)(2,1)S(1)}, bf16[16384]{0:T(1024)(128)(2,1)S(1)}, u32[]{:S(2)}, u32[]{:S(2)}) %collective-permute-start.3) | collective-permute-done | bytes 32800 | tf_op jit(solution)/shard_map/ppermute | solution.py:78
  41.7 0.1 fusion.20
  41.8 0.2 broadcast_in_dim.4
  42.0 18.6 %all_to_all.11 = bf16[32,128,128]{2,1,0:T(8,128)(2,1)S(1)} all-to-all(bf16[32,128,128]{2,1,0:T(8,128)(2,1)S(1)} %broadcast_in_dim.4), channel_id=1, replica_groups={{0,16,32,48,4,20,36,52,8,24,40,56,12,28,44,60,1,17,33,49,5,21,37,53,9,2..., dimensions={0} | all-to-all | bytes 2097152 | tf_op jit(solution)/shard_map/all_to_all | solution.py:38
  60.6 3.7 %collective-permute-start.4 = (bf16[32,128,128]{2,1,0:T(8,128)(2,1)S(1)}, bf16[32,128,128]{2,1,0:T(8,128)(2,1)S(1)}, u32[]{:S(2)}, u32[]{:S(2)}) collective-permute-start(bf16[32,128,128]{2,1,0:T(8,128)(2,1)S(1)} %all_to_all.11), channel_id=1, source_target_pairs={{0,2},{2,0},{1,3},{3,1},{4,6},{6,4},{5,7},{7,5},{8,10},{10,8},{9,1... | collective-permute-start | bytes 3145736 | tf_op jit(solution)/shard_map/ppermute | solution.py:85
  64.3 0.7 %multiply_subtract_fusion = (f32[16384]{0:T(1024)}, f32[16384]{0:T(1024)}, f32[16384]{0:T(1024)}) fusion(f32[16384]{0:T(1024)S(1)} %copy-done.1, f32[16384]{0:T(1024)S(1)} %get-tuple-element.37, f32[16384]{0:T(1024)S(1)} %copy-done.3, f32[16384]{0:T(1024)S(1)} %copy-done.2), kind=kLoop, calls=%fused_computation.38 | loop fusion | flops 245760 | bytes 458752 | tf_op jit(solution)/shard_map/sub | solution.py:58
  65.0 1.6 %collective-permute-done.4 = bf16[32,128,128]{2,1,0:T(8,128)(2,1)S(1)} collective-permute-done((bf16[32,128,128]{2,1,0:T(8,128)(2,1)S(1)}, bf16[32,128,128]{2,1,0:T(8,128)(2,1)S(1)}, u32[]{:S(2)}, u32[]{:S(2)}) %collective-permute-start.4) | collective-permute-done | bytes 1048608 | tf_op jit(solution)/shard_map/ppermute | solution.py:85
  66.6 0.1 broadcast_select_fusion.1
  66.7 0.1 reverse_bitcast_fusion
  66.8 0.1 copy.17
  66.9 0.1 copy.16
  67.0 0.2 pad_maximum_fusion
  67.2 1.5 %copy.18 = bf16[16,2,2,128,128]{4,3,2,1,0:T(8,128)(2,1)} copy(bf16[16,2,2,128,128]{4,3,2,0,1:T(8,128)(2,1)S(1)} %pad_maximum_fusion) | data formatting | bytes 4194304 | tf_op jit(solution)/shard_map/stack | solution.py:50
  (6 shorter events, 0.0 us)
Async XLA Ops:
  2.4 5.6 %collective-permute-start = (bf16[16,2,128,128]{3,2,1,0:T(8,128)(2,1)S(1)}, bf16[16,2,128,128]{3,2,1,0:T(8,128)(2,1)S(1)}, u32[]{:S(2)}, u32[]{:S(2)}) collective-permute-start(bf16[16,2,128,128]{3,2,1,0:T(8,128)(2,1)S(1)} %fusion.7), channel_id=1, source_target_pairs={{0,2},{2,0},{1,3},{3,1},{4,6},{6,4},{5,7},{7,5},{8,10},{10,8},{9,1... | collective-permute-start | bytes 3145736 | tf_op jit(solution)/shard_map/ppermute | solution.py:67
  8.9 20.4 %copy-start = (f32[1,16384]{1,0:T(1,128)S(1)}, f32[1,16384]{1,0:T(1,128)}, u32[]{:S(2)}) copy-start(f32[1,16384]{1,0:T(1,128)} %param.8) | copy-start | bytes 196612
  8.9 32.8 %copy-start.1 = (f32[16384]{0:T(1024)S(1)}, f32[16384]{0:T(1024)}, u32[]{:S(2)}) copy-start(f32[16384]{0:T(1024)} %param.9) | copy-start | bytes 196612
  8.9 32.8 %copy-start.2 = (f32[16384]{0:T(1024)S(1)}, f32[16384]{0:T(1024)}, u32[]{:S(2)}) copy-start(f32[16384]{0:T(1024)} %param.11) | copy-start | bytes 196612
  8.9 32.7 %copy-start.3 = (f32[16384]{0:T(1024)S(1)}, f32[16384]{0:T(1024)}, u32[]{:S(2)}) copy-start(f32[16384]{0:T(1024)} %param.10) | copy-start | bytes 196612
  29.3 10.2 %collective-permute-start.1 = (bf16[16384]{0:T(1024)(128)(2,1)S(1)}, bf16[16384]{0:T(1024)(128)(2,1)S(1)}, u32[]{:S(2)}, u32[]{:S(2)}) collective-permute-start(bf16[16384]{0:T(1024)(128)(2,1)S(1)} %fusion.21), channel_id=1, source_target_pairs={{0,128},{2,130},{64,192},{66,194},{128,0},{130,2},{192,64},{194,66... | collective-permute-start | bytes 98312 | tf_op jit(solution)/shard_map/ppermute | solution.py:78
  36.4 3.7 %collective-permute-start.2 = (bf16[16384]{0:T(1024)(128)(2,1)S(1)}, bf16[16384]{0:T(1024)(128)(2,1)S(1)}, u32[]{:S(2)}, u32[]{:S(2)}) collective-permute-start(bf16[16384]{0:T(1024)(128)(2,1)S(1)} %fusion.21), channel_id=1, source_target_pairs={{0,64},{2,194},{64,128},{66,2},{128,192},{130,66},{192,0},{194,130... | collective-permute-start | bytes 98312 | tf_op jit(solution)/shard_map/ppermute | solution.py:78
  36.4 5.2 %collective-permute-start.3 = (bf16[16384]{0:T(1024)(128)(2,1)S(1)}, bf16[16384]{0:T(1024)(128)(2,1)S(1)}, u32[]{:S(2)}, u32[]{:S(2)}) collective-permute-start(bf16[16384]{0:T(1024)(128)(2,1)S(1)} %fusion.21), channel_id=1, source_target_pairs={{0,192},{2,66},{64,0},{66,130},{128,64},{130,194},{192,128},{194,2... | collective-permute-start | bytes 98312 | tf_op jit(solution)/shard_map/ppermute | solution.py:78
  60.6 6.0 %collective-permute-start.4 = (bf16[32,128,128]{2,1,0:T(8,128)(2,1)S(1)}, bf16[32,128,128]{2,1,0:T(8,128)(2,1)S(1)}, u32[]{:S(2)}, u32[]{:S(2)}) collective-permute-start(bf16[32,128,128]{2,1,0:T(8,128)(2,1)S(1)} %all_to_all.11), channel_id=1, source_target_pairs={{0,2},{2,0},{1,3},{3,1},{4,6},{6,4},{5,7},{7,5},{8,10},{10,8},{9,1... | collective-permute-start | bytes 3145736 | tf_op jit(solution)/shard_map/ppermute | solution.py:85

commit v7 on v5

--- a/solution.py
+++ b/solution.py
@@ -25,8 +25,11 @@
     return jnp.where(jnp.abs(code) > 2.0, code * (1.0 / 1024.0) + jnp.clip(code, -1.0, 1.0), code)
 
 
-REDUCE = [(x, y, z) for z, y, x in itertools.product(range(2), range(4), range(4))]
-GATHER = [(x, y, z) for z, y, x in itertools.product(range(2), range(4), range(4))]
+REDUCE = [
+    (2 * x1 + (x0 ^ x1), 2 * y1 + (y0 ^ y1), z)
+    for y0, z, x0, y1, x1 in itertools.product((0, 1), repeat=5)
+]
+GATHER = [(x, y, z) for z, x, y in itertools.product(range(2), range(4), range(4))]
 
 
 def exchange(blocks, chips):
@@ -38,15 +41,21 @@
     return lax.all_to_all(blocks, ("cuts",) + OWN, 0, 0, axis_index_groups=groups, tiled=True)
 
 
+def gray(blocks, axis):
+    low, high = jnp.split(blocks, 2, axis)
+    return jnp.concatenate([low, jnp.flip(high, axis)], axis)
+
+
 def outgoing(own, other, core):
     code = coded(own.astype(jnp.float32) + other.astype(jnp.float32)).reshape(4, 4, 2, *TILE)
-    code = code.transpose(2, 1, 0, 3, 4)
-    return (jnp.flip(code, (0, 1, 2)) if core else code).reshape(32, *TILE)
+    code = gray(gray(code, 0), 1).reshape(2, 2, 2, 2, 2, *TILE)
+    code = code.transpose(3, 4, 1, 2, 0, 5, 6)
+    return (jnp.flip(code, (0, 1, 2, 3, 4)) if core else code).reshape(32, *TILE)
 
 
 def in_place(first, second):
     first, second = first.reshape(2, 4, 4, *TILE), jnp.flip(second.reshape(2, 4, 4, *TILE), (0, 1, 2))
-    first, second = (half.transpose(2, 1, 0, 3, 4).reshape(16, 2, *TILE) for half in (first, second))
+    first, second = (half.transpose(1, 2, 0, 3, 4).reshape(16, 2, *TILE) for half in (first, second))
     return jnp.stack([first, second], axis=1)
 
 

time: 68.9 us -> 69.4 us (level)
  blocking collectives: 38 us -> 40.2 us
  starting transfers between devices: 18.5 us -> 16.4 us
    all_to_all x2, blocking collectives: 38 us -> 40.2 us  [exchange(): lax.all_to_all(blocks, ('cuts',) + OWN, 0, 0, axis_index_groups=groups, t...]
    ppermute x1, starting transfers between devices: 4.47 us -> 3 us  [on_device(): theirs = lax.ppermute(mine, 'core', SWAP)]
where the time goes in v7:
time: 69.4 us; the launch traced here: 69.2 us
  blocking collectives  40.2 us (58%)
  starting transfers between devices  16.4 us (24%)
  local copies, waits for them, and re-layouts  5.72 us (8%)
  other arithmetic  3.23 us (5%)
  waiting for transfers between devices  2.76 us (4%)
  between operations  0.75 us (1%)
    all_to_all x2, blocking collectives, exchange(): lax.all_to_all(blocks, ('cuts',) + OWN, 0, 0, axis_index_groups=groups, t...  40.2 us
    ppermute x3, starting transfers between devices, on_device(): sents = [lax.ppermute(narrow, ('cuts', 'core'), turn) for turn in TURNS]  10.1 us
    convert_element_type x2, local copies, waits for them, and re-layouts, on_device(): lax.dynamic_index_in_dim(blocks, which, 1, False).astype(jnp.bfloat16)  3.51 us
    ppermute x1, starting transfers between devices, on_device(): other = lax.ppermute(leaving, 'core', SWAP)  3.33 us
    ppermute x1, starting transfers between devices, on_device(): theirs = lax.ppermute(mine, 'core', SWAP)  3 us
    ppermute x1, waiting for transfers between devices, on_device(): theirs = lax.ppermute(mine, 'core', SWAP)  1.59 us
    another operation x1, local copies, waits for them, and re-layouts, in_place(): return jnp.stack([first, second], axis=1)  1.46 us
  transfers between devices with their start and end apart: 5, of which 3 were waited for; matrix products, arithmetic and copies ran while one was open for 5% of the time, Pallas kernels for 0%

profile of v7, /device:TPU:1, one launch (start us, length us, event | category | flops | bytes accessed | tf_op | source)
XLA Modules:
  0.0 69.2 jit_solution(13018567734056384764)
XLA Ops:
  0.6 1.8 %fusion.9 = bf16[16,2,128,128]{3,2,1,0:T(8,128)(2,1)S(1)} fusion(f32[16,2,2,128,128]{4,3,2,1,0:T(8,128)} %bitcast.58, s32[]{:T(128)S(6)} %select_n.31), kind=kLoop, calls=%fused_computation.28 | loop fusion | bytes 2097156 | tf_op jit(solution)/shard_map/convert_element_type | solution.py:74
  2.4 3.3 %collective-permute-start = (bf16[16,2,128,128]{3,2,1,0:T(8,128)(2,1)S(1)}, bf16[16,2,128,128]{3,2,1,0:T(8,128)(2,1)S(1)}, u32[]{:S(2)}, u32[]{:S(2)}) collective-permute-start(bf16[16,2,128,128]{3,2,1,0:T(8,128)(2,1)S(1)} %fusion.9), channel_id=1, source_target_pairs={{0,2},{2,0},{1,3},{3,1},{4,6},{6,4},{5,7},{7,5},{8,10},{10,8},{9,1... | collective-permute-start | bytes 3145736 | tf_op jit(solution)/shard_map/ppermute | solution.py:76
  5.7 1.8 %fusion.10 = bf16[16,2,128,128]{3,2,1,0:T(8,128)(2,1)S(1)} fusion(f32[16,2,2,128,128]{4,3,2,1,0:T(8,128)} %bitcast.59, s32[]{:T(128)S(6)} %select_n.32), kind=kLoop, calls=%fused_computation.29 | loop fusion | bytes 2097156 | tf_op jit(solution)/shard_map/convert_element_type | solution.py:74
  7.5 0.5 collective-permute-done
  8.0 1.3 %conditional.1 = (bf16[32,128,128]{2,1,0:T(8,128)(2,1)S(1)}) conditional(s32[]{:T(128)} %convert_element_type.51, (bf16[16,2,128,128]{3,2,1,0:T(8,128)(2,1)S(1)}, bf16[16,2,128,128]{3,2,1,0:T(8,128)(2,1)S(1)}) %tuple.18, (bf16[16,2,128,128]{3,2,1,0:T(8,128)(2,1)S(1)}, bf16[16,2,128,128]{3,2,1,0:T(8,128)(2,1)S(1)}) %tuple.18), branch_computations={%region_0.1_spmd, %region_1.2_spmd} | conditional | flops 5767168 | bytes 15728648 | solution.py:80
  8.0 0.6 fusion.1
  8.6 0.1 fusion.25
  8.8 0.1 fusion.2
  9.0 0.1 pad_maximum_fusion
  9.1 0.1 rev.18
  9.2 0.1 copy.10
  9.3 0.0 copy-start
  9.3 0.0 copy-start.1
  9.3 0.0 copy-start.2
  9.3 0.0 copy-start.3
  9.3 19.8 %all_to_all.10 = bf16[32,128,128]{2,1,0:T(8,128)(2,1)S(1)} all-to-all(bf16[32,128,128]{2,1,0:T(8,128)(2,1)S(1)} %get-tuple-element.55), channel_id=1, replica_groups={{0,48,12,60,16,32,28,44,1,49,13,61,17,33,29,45,4,52,8,56,20,36,24,40,5,..., dimensions={0} | all-to-all | bytes 2097152 | tf_op jit(solution)/shard_map/all_to_all | solution.py:41
  29.2 0.5 fusion.8
  29.7 3.1 %collective-permute-start.1 = (bf16[16384]{0:T(1024)(128)(2,1)S(1)}, bf16[16384]{0:T(1024)(128)(2,1)S(1)}, u32[]{:S(2)}, u32[]{:S(2)}) collective-permute-start(bf16[16384]{0:T(1024)(128)(2,1)S(1)} %fusion.23), channel_id=1, source_target_pairs={{0,192},{2,66},{64,0},{66,130},{128,64},{130,194},{192,128},{194,2... | collective-permute-start | bytes 98312 | tf_op jit(solution)/shard_map/ppermute | solution.py:87
  32.8 4.6 %collective-permute-start.2 = (bf16[16384]{0:T(1024)(128)(2,1)S(1)}, bf16[16384]{0:T(1024)(128)(2,1)S(1)}, u32[]{:S(2)}, u32[]{:S(2)}) collective-permute-start(bf16[16384]{0:T(1024)(128)(2,1)S(1)} %fusion.23), channel_id=1, source_target_pairs={{0,128},{2,130},{64,192},{66,194},{128,0},{130,2},{192,64},{194,66... | collective-permute-start | bytes 98312 | tf_op jit(solution)/shard_map/ppermute | solution.py:87
  37.4 2.4 %collective-permute-start.3 = (bf16[16384]{0:T(1024)(128)(2,1)S(1)}, bf16[16384]{0:T(1024)(128)(2,1)S(1)}, u32[]{:S(2)}, u32[]{:S(2)}) collective-permute-start(bf16[16384]{0:T(1024)(128)(2,1)S(1)} %fusion.23), channel_id=1, source_target_pairs={{0,64},{2,194},{64,128},{66,2},{128,192},{130,66},{192,0},{194,130... | collective-permute-start | bytes 98312 | tf_op jit(solution)/shard_map/ppermute | solution.py:87
  39.8 0.7 %multiply_subtract_fusion.1 = f32[1,16384]{1,0:T(1,128)} fusion(f32[1,16384]{1,0:T(1,128)S(1)} %bitcast.60, f32[1,16384]{1,0:T(1,128)S(1)} %copy-done), kind=kLoop, calls=%fused_computation.50 | loop fusion | flops 98304 | bytes 196608 | tf_op jit(solution)/shard_map/sub | solution.py:85
  40.6 0.6 collective-permute-done.3
  41.2 0.1 fusion.22
  41.3 0.2 broadcast_in_dim.4
  41.5 20.4 %all_to_all.11 = bf16[32,128,128]{2,1,0:T(8,128)(2,1)S(1)} all-to-all(bf16[32,128,128]{2,1,0:T(8,128)(2,1)S(1)} %broadcast_in_dim.4), channel_id=1, replica_groups={{0,4,8,12,16,20,24,28,32,36,40,44,48,52,56,60,1,5,9,13,17,21,25,29,33,3..., dimensions={0} | all-to-all | bytes 2097152 | tf_op jit(solution)/shard_map/all_to_all | solution.py:41
  62.0 3.0 %collective-permute-start.4 = (bf16[32,128,128]{2,1,0:T(8,128)(2,1)S(1)}, bf16[32,128,128]{2,1,0:T(8,128)(2,1)S(1)}, u32[]{:S(2)}, u32[]{:S(2)}) collective-permute-start(bf16[32,128,128]{2,1,0:T(8,128)(2,1)S(1)} %all_to_all.11), channel_id=1, source_target_pairs={{0,2},{2,0},{1,3},{3,1},{4,6},{6,4},{5,7},{7,5},{8,10},{10,8},{9,1... | collective-permute-start | bytes 3145736 | tf_op jit(solution)/shard_map/ppermute | solution.py:94
  65.0 0.7 %multiply_subtract_fusion = (f32[16384]{0:T(1024)}, f32[16384]{0:T(1024)}, f32[16384]{0:T(1024)}) fusion(f32[16384]{0:T(1024)S(1)} %copy-done.1, f32[16384]{0:T(1024)S(1)} %get-tuple-element.37, f32[16384]{0:T(1024)S(1)} %copy-done.3, f32[16384]{0:T(1024)S(1)} %copy-done.2), kind=kLoop, calls=%fused_computation.46 | loop fusion | flops 245760 | bytes 458752 | tf_op jit(solution)/shard_map/sub | solution.py:67
  65.6 1.6 %collective-permute-done.4 = bf16[32,128,128]{2,1,0:T(8,128)(2,1)S(1)} collective-permute-done((bf16[32,128,128]{2,1,0:T(8,128)(2,1)S(1)}, bf16[32,128,128]{2,1,0:T(8,128)(2,1)S(1)}, u32[]{:S(2)}, u32[]{:S(2)}) %collective-permute-start.4) | collective-permute-done | bytes 1048608 | tf_op jit(solution)/shard_map/ppermute | solution.py:94
  67.2 0.1 broadcast_select_fusion.1
  67.4 0.1 rev.22
  67.5 0.2 pad_maximum_fusion.4
  67.7 1.5 %copy.14 = bf16[16,2,2,128,128]{4,3,2,1,0:T(8,128)(2,1)} copy(bf16[16,2,2,128,128]{4,3,0,2,1:T(8,128)(2,1)S(1)} %pad_maximum_fusion.4) | data formatting | bytes 4194304 | tf_op jit(solution)/shard_map/stack | solution.py:59
  (9 shorter events, 0.1 us)
Async XLA Ops:
  2.4 5.6 %collective-permute-start = (bf16[16,2,128,128]{3,2,1,0:T(8,128)(2,1)S(1)}, bf16[16,2,128,128]{3,2,1,0:T(8,128)(2,1)S(1)}, u32[]{:S(2)}, u32[]{:S(2)}) collective-permute-start(bf16[16,2,128,128]{3,2,1,0:T(8,128)(2,1)S(1)} %fusion.9), channel_id=1, source_target_pairs={{0,2},{2,0},{1,3},{3,1},{4,6},{6,4},{5,7},{7,5},{8,10},{10,8},{9,1... | collective-permute-start | bytes 3145736 | tf_op jit(solution)/shard_map/ppermute | solution.py:76
  9.3 20.4 %copy-start = (f32[1,16384]{1,0:T(1,128)S(1)}, f32[1,16384]{1,0:T(1,128)}, u32[]{:S(2)}) copy-start(f32[1,16384]{1,0:T(1,128)} %param.8) | copy-start | bytes 196612
  9.3 31.9 %copy-start.1 = (f32[16384]{0:T(1024)S(1)}, f32[16384]{0:T(1024)}, u32[]{:S(2)}) copy-start(f32[16384]{0:T(1024)} %param.9) | copy-start | bytes 196612
  9.3 31.9 %copy-start.2 = (f32[16384]{0:T(1024)S(1)}, f32[16384]{0:T(1024)}, u32[]{:S(2)}) copy-start(f32[16384]{0:T(1024)} %param.11) | copy-start | bytes 196612
  9.3 31.9 %copy-start.3 = (f32[16384]{0:T(1024)S(1)}, f32[16384]{0:T(1024)}, u32[]{:S(2)}) copy-start(f32[16384]{0:T(1024)} %param.10) | copy-start | bytes 196612
  29.7 10.8 %collective-permute-start.1 = (bf16[16384]{0:T(1024)(128)(2,1)S(1)}, bf16[16384]{0:T(1024)(128)(2,1)S(1)}, u32[]{:S(2)}, u32[]{:S(2)}) collective-permute-start(bf16[16384]{0:T(1024)(128)(2,1)S(1)} %fusion.23), channel_id=1, source_target_pairs={{0,192},{2,66},{64,0},{66,130},{128,64},{130,194},{192,128},{194,2... | collective-permute-start | bytes 98312 | tf_op jit(solution)/shard_map/ppermute | solution.py:87
  32.8 7.8 %collective-permute-start.2 = (bf16[16384]{0:T(1024)(128)(2,1)S(1)}, bf16[16384]{0:T(1024)(128)(2,1)S(1)}, u32[]{:S(2)}, u32[]{:S(2)}) collective-permute-start(bf16[16384]{0:T(1024)(128)(2,1)S(1)} %fusion.23), channel_id=1, source_target_pairs={{0,128},{2,130},{64,192},{66,194},{128,0},{130,2},{192,64},{194,66... | collective-permute-start | bytes 98312 | tf_op jit(solution)/shard_map/ppermute | solution.py:87
  37.4 3.8 %collective-permute-start.3 = (bf16[16384]{0:T(1024)(128)(2,1)S(1)}, bf16[16384]{0:T(1024)(128)(2,1)S(1)}, u32[]{:S(2)}, u32[]{:S(2)}) collective-permute-start(bf16[16384]{0:T(1024)(128)(2,1)S(1)} %fusion.23), channel_id=1, source_target_pairs={{0,64},{2,194},{64,128},{66,2},{128,192},{130,66},{192,0},{194,130... | collective-permute-start | bytes 98312 | tf_op jit(solution)/shard_map/ppermute | solution.py:87
  62.0 5.3 %collective-permute-start.4 = (bf16[32,128,128]{2,1,0:T(8,128)(2,1)S(1)}, bf16[32,128,128]{2,1,0:T(8,128)(2,1)S(1)}, u32[]{:S(2)}, u32[]{:S(2)}) collective-permute-start(bf16[32,128,128]{2,1,0:T(8,128)(2,1)S(1)} %all_to_all.11), channel_id=1, source_target_pairs={{0,2},{2,0},{1,3},{3,1},{4,6},{6,4},{5,7},{7,5},{8,10},{10,8},{9,1... | collective-permute-start | bytes 3145736 | tf_op jit(solution)/shard_map/ppermute | solution.py:94
